TPU v7x, 256 devices: a whole 4x4x8 slice. The times are simulated.
256 devices in a mesh: sites: 64 (over z, y, core), rep: 4 (over x).
Axes of the slice: x: 4, y: 4, z: 8, core: 2. Of those that a mesh axis runs over, the one named last changes fastest.
Arguments:
- coords: float32 [2, 131072], P(None, 'sites'), may hold values from 0 to 53200, as said below
- scale: float32 [131072], P('sites'), may hold values from 0.5 to 2
- nugget: float32 [131072], P('sites'), may hold values from 0.2 to 1
- right_side: float32 [32, 131072], P(None, 'sites'), may hold values from -6 to 6
- site_order: int32 [131072], P('sites'), may hold values from 0 to 131071, as said below
- pair_list: int32 [2, 4608], P(None, ('sites', 'rep')), may hold values from 0 to 511, as said below
- pair_count: int32 [256], P(('sites', 'rep')), may hold values from 2 to 18, as said below
Outputs:
- solution_field: float32 [32, 131072], P(None, 'sites')
- residual: float32 [32, 131072], P(None, 'sites')
Inputs may be any that keep to these rules, and one draw needn't show every extreme that they name: `site_order`: within the 2048 positions of each index of sites, a permutation of those same positions' indices. `pair_list`: each device's 18 slots hold its listed pairs first and (0, 0) after them. A listed pair has row <= column <= row + 8, column below 512, its row block among the 8 blocks of the device's index along sites; every pair of blocks with sites closer than 200 km is listed once, and no pair is listed twice. `pair_count`: every row block's own pair is listed; some devices list 18 pairs. `coords`: sites of block b lie in a band of east coordinates of its own; bands follow each other without gaps.
All inputs are finite; a program needn't handle non-finite values.
Results may differ from a plain program's by a relative error of at most 0.0003.
Values sent between devices are 32-bit elements; how exact they have to be, the bound alone decides.
A program may use at most 64 MiB of HBM per device.

v0:
```python
import jax
import jax.numpy as jnp
from jax import lax
from jax.sharding import PartitionSpec as P

BLK = 256
ITERS = 3


RANGE_KM = 200.0
HIGHEST_PRECISION = lax.Precision.HIGHEST


def passed_along(array, axis, by):
    size = lax.axis_size(axis)
    pairs = [(i, i + by) for i in range(size) if 0 <= i + by < size]
    return lax.ppermute(array, axis, pairs)


def taper_tile(row_geo, col_geo):
    delta_east = row_geo[0][:, None] - col_geo[0][None, :]
    delta_north = row_geo[1][:, None] - col_geo[1][None, :]
    distance = jnp.sqrt(delta_east * delta_east + delta_north * delta_north)
    ratio = jnp.minimum(distance / RANGE_KM, 1.0)
    remain = 1.0 - ratio
    square = remain * remain
    return row_geo[2][:, None] * col_geo[2][None, :] * (square * square) * (1.0 + 4.0 * ratio)


def tile_terms(vectors, geo, row_start, col_start):
    tile = taper_tile(
        lax.dynamic_slice_in_dim(geo, row_start, BLK, 1),
        lax.dynamic_slice_in_dim(geo, col_start, BLK, 1),
    )
    to_row = lax.dot_general(
        lax.dynamic_slice_in_dim(vectors, col_start, BLK, 1),
        tile,
        (((1,), (1,)), ((), ())),
        precision=HIGHEST_PRECISION,
        preferred_element_type=jnp.float32,
    )
    to_col = jnp.dot(
        lax.dynamic_slice_in_dim(vectors, row_start, BLK, 1),
        tile,
        precision=HIGHEST_PRECISION,
        preferred_element_type=jnp.float32,
    )
    return (to_row, to_col)


def add_block(accumulated, start, term):
    return lax.dynamic_update_slice_in_dim(
        accumulated, lax.dynamic_slice_in_dim(accumulated, start, BLK, 1) + term, start, 1
    )


def local(coords, scale, nugget, right_side, site_order, pair_list, pair_count):
    group_width = right_side.shape[1]
    rep_count = lax.axis_size("rep")
    share_width = group_width // rep_count
    rep_place = lax.axis_index("rep")
    local_index = site_order - lax.axis_index("sites") * group_width
    geo = jnp.concatenate(
        [jnp.take(coords, local_index, axis=1), jnp.take(scale, local_index)[None, :]], axis=0
    )
    damping = jnp.take(nugget, local_index)
    ordered = jnp.take(right_side, local_index, axis=1)
    geo_ahead = passed_along(geo, "sites", -1)
    wide_geo = jnp.concatenate([geo, geo_ahead], axis=1)
    first_block = lax.axis_index("sites") * (group_width // BLK)
    row_blocks = pair_list[0] - first_block
    col_blocks = pair_list[1] - first_block
    pair_total = pair_count[0]

    def own_part(array):
        return lax.dynamic_slice_in_dim(array, rep_place * share_width, share_width, array.ndim - 1)

    def counted_part(array):
        return own_part(array)

    def local_sum(first_vec, second_vec):
        return jnp.sum(counted_part(first_vec) * counted_part(second_vec), axis=1)

    def squares(residual):
        return lax.psum(local_sum(residual, residual), ("sites", "rep"))

    solution = jnp.zeros_like(ordered)
    residual = ordered
    direction = ordered
    norm_now = squares(residual)
    for iteration in range(ITERS):
        ahead_blocks = passed_along(direction, "sites", -1)
        widened = jnp.concatenate([direction, ahead_blocks], axis=1)

        def add_pair(slot_step, accumulated):
            row_block = row_blocks[slot_step]
            col_block = col_blocks[slot_step]
            row_start = row_block * BLK
            col_start = col_block * BLK
            distinct = (row_block != col_block).astype(jnp.float32)
            to_row, to_col = tile_terms(widened, wide_geo, row_start, col_start)
            accumulated = add_block(accumulated, row_start, to_row)
            return add_block(accumulated, col_start, to_col * distinct)

        accumulated = lax.fori_loop(
            0, pair_total, add_pair, jnp.zeros((widened.shape[0], 2 * group_width), jnp.float32)
        )
        passed_down = passed_along(accumulated[:, group_width:], "sites", 1)
        partial_terms = accumulated[:, :group_width] + passed_down
        image = lax.psum(partial_terms, "rep") + damping[None, :] * direction
        alpha = norm_now / lax.psum(local_sum(direction, image), ("sites", "rep"))
        solution = solution + alpha[:, None] * direction
        residual = residual - alpha[:, None] * image
        norm_next = squares(residual)
        direction = residual + (norm_next / norm_now)[:, None] * direction
        norm_now = norm_next
    return (solution, residual)


def solution(mesh):
    in_specs = (
        P(None, "sites"),
        P("sites"),
        P("sites"),
        P(None, "sites"),
        P("sites"),
        P(None, ("sites", "rep")),
        P(("sites", "rep")),
    )
    out_specs = (P(None, "sites"), P(None, "sites"))
    return jax.shard_map(local, mesh=mesh, in_specs=in_specs, out_specs=out_specs, check_vma=False)
```

profile of v0, /device:TPU:1, one launch (start us, length us, event | category | flops | bytes accessed | tf_op | source)
XLA Modules:
  0.0 919.4 jit_solution(16328909343659178699)
XLA Ops:
  7.9 11.8 %gather_fusion.3 = f32[2048]{0:T(1024)S(1)} fusion(f32[2048]{0:T(1024)S(1)} %copy-done, s32[2048]{0:T(1024)S(1)} %fusion.95), kind=kCustom, calls=%fused_computation.1.clone | custom fusion | bytes 24576 | tf_op jit(solution)/shard_map/jit(_take)/gather | solution.py:66
  20.8 5.5 gather_fusion.1
  27.3 11.8 %gather_fusion.2 = f32[2048]{0:T(1024)S(1)} fusion(f32[2048]{0:T(1024)S(1)} %copy-done.1, s32[2048]{0:T(1024)S(1)} %fusion.95), kind=kCustom, calls=%fused_computation.clone | custom fusion | bytes 24576 | tf_op jit(solution)/shard_map/jit(_take)/gather | solution.py:64
  39.1 5.2 collective-permute-start.1
  44.6 5.5 gather_fusion
  50.5 1.9 collective-permute-start
  52.5 5.7 collective-permute-done
  58.2 46.9 %while.30 = (s32[]{:T(128)}, f32[32,4096]{1,0:T(8,128)S(1)}, s32[]{:T(128)}, s32[18]{0:T(128)S(1)}, s32[18]{0:T(128)S(1)}, /*index=5*/f32[32,4096]{1,0:T(8,128)S...) while((s32[]{:T(128)}, f32[32,4096]{1,0:T(8,128)S(1)}, ...), condition=%wide.region_3.5_spmd, body=%wide.region_2.4_spmd.sunk | while | flops 52322320 | bytes 221541 | solution.py:105
  105.1 1.9 collective-permute-start.2
  107.1 7.7 collective-permute-done.2
  115.6 94.5 %all-reduce.5.cloned.1.call-done = f32[32,2048]{1,0:T(8,128)} async-done(((f32[32,2048]{1,0:T(8,128)}), f32[32,2048]{1,0:T(8,128)}) %all-reduce.5.cloned.1.call-update) | async-done | bytes 262160 | tf_op jit(solution)/shard_map/psum | solution.py:110
  210.1 1.0 multiply_add_fusion.5
  211.3 78.0 %all-reduce = (f32[32]{0:T(128)S(1)}, f32[32]{0:T(128)S(1)}) all-reduce(f32[32]{0:T(128)S(1)} %get-tuple-element.169, f32[32]{0:T(128)S(1)} %get-tuple-element.168), channel_id=1, replica_groups=mesh['sites'=64,'rep'=4] {'sites','rep'}, use_global_device_ids=true, to_apply=%region_1.2 | all-reduce | flops 64 | bytes 512 | tf_op jit(solution)/shard_map/psum | solution.py:85
  289.5 73.6 %psum.66 = f32[32]{0:T(128)S(1)} all-reduce(f32[32]{0:T(128)S(1)} %multiply_reduce_fusion.3), channel_id=1, replica_groups=mesh['sites'=64,'rep'=4] {'sites','rep'}, use_global_device_ids=true, to_apply=%region_8.10 | all-reduce | flops 32 | bytes 256 | tf_op jit(solution)/shard_map/psum | solution.py:85
  363.2 2.6 collective-permute-start.3
  365.8 5.1 collective-permute-done.3
  371.0 46.9 %while.31 = (s32[]{:T(128)}, f32[32,4096]{1,0:T(8,128)S(1)}, s32[]{:T(128)}, s32[18]{0:T(128)S(1)}, s32[18]{0:T(128)S(1)}, /*index=5*/f32[32,4096]{1,0:T(8,128)S...) while((s32[]{:T(128)}, f32[32,4096]{1,0:T(8,128)S(1)}, ...), condition=%wide.region_10.12_spmd, body=%wide.region_9.11_spmd.sunk | while | flops 52322320 | bytes 221541 | solution.py:105
  417.9 1.9 collective-permute-start.4
  419.8 8.3 collective-permute-done.4
  429.0 92.5 %all-reduce.7.cloned.1.call-done = f32[32,2048]{1,0:T(8,128)} async-done(((f32[32,2048]{1,0:T(8,128)}), f32[32,2048]{1,0:T(8,128)}) %all-reduce.7.cloned.1.call-update) | async-done | bytes 262160 | tf_op jit(solution)/shard_map/psum | solution.py:110
  521.5 1.0 multiply_add_fusion.3
  522.6 78.0 %psum.68 = f32[32]{0:T(128)S(1)} all-reduce(f32[32]{0:T(128)S(1)} %multiply_reduce_fusion.2), channel_id=1, replica_groups=mesh['sites'=64,'rep'=4] {'sites','rep'}, use_global_device_ids=true, to_apply=%region_13.15 | all-reduce | flops 32 | bytes 256 | tf_op jit(solution)/shard_map/psum | solution.py:111
  600.8 73.6 %psum.69 = f32[32]{0:T(128)S(1)} all-reduce(f32[32]{0:T(128)S(1)} %multiply_reduce_fusion.1), channel_id=1, replica_groups=mesh['sites'=64,'rep'=4] {'sites','rep'}, use_global_device_ids=true, to_apply=%region_15.17 | all-reduce | flops 32 | bytes 256 | tf_op jit(solution)/shard_map/psum | solution.py:85
  674.5 2.6 collective-permute-start.5
  677.1 5.1 collective-permute-done.5
  682.3 46.9 %while.32 = (s32[]{:T(128)}, f32[32,4096]{1,0:T(8,128)S(1)}, s32[]{:T(128)}, s32[18]{0:T(128)S(1)}, s32[18]{0:T(128)S(1)}, /*index=5*/f32[32,4096]{1,0:T(8,128)S...) while((s32[]{:T(128)}, f32[32,4096]{1,0:T(8,128)S(1)}, ...), condition=%wide.region_17.19_spmd, body=%wide.region_16.18_spmd.sunk | while | flops 52322320 | bytes 221541 | solution.py:105
  729.2 1.9 collective-permute-start.6
  731.1 8.3 collective-permute-done.6
  740.2 92.6 %all-reduce.9.cloned.1.call-done = f32[32,2048]{1,0:T(8,128)} async-done(((f32[32,2048]{1,0:T(8,128)}), f32[32,2048]{1,0:T(8,128)}) %all-reduce.9.cloned.1.call-update) | async-done | bytes 262160 | tf_op jit(solution)/shard_map/psum | solution.py:110
  832.8 1.0 multiply_add_fusion.1
  833.9 78.0 %psum.71 = f32[32]{0:T(128)S(1)} all-reduce(f32[32]{0:T(128)S(1)} %multiply_reduce_fusion), channel_id=1, replica_groups=mesh['sites'=64,'rep'=4] {'sites','rep'}, use_global_device_ids=true, to_apply=%region_20.22 | all-reduce | flops 32 | bytes 256 | tf_op jit(solution)/shard_map/psum | solution.py:111
  911.9 0.9 multiply_subtract_fusion
  (178 shorter events, 64.7 us)
Async XLA Ops:
  7.2 0.7 copy-start
  7.2 0.7 copy-start.3
  7.2 202.9 %all-reduce.5.cloned.1.call-start = ((), (), s32[]{:S(2)}) async-start(), calls=%async_computation | async-start | bytes 524288 | tf_op jit(solution)/shard_map/psum | solution.py:110
  19.7 0.7 copy-start.4
  26.6 0.7 copy-start.1
  27.3 17.0 %copy-start.2 = (f32[32,2048]{1,0:T(8,128)S(1)}, f32[32,2048]{1,0:T(8,128)}, u32[]{:S(2)}) copy-start(f32[32,2048]{1,0:T(8,128)} %param.18) | copy-start | bytes 786436
  39.1 13.3 %collective-permute-start.1 = (f32[3,2048]{1,0:T(4,128)S(1)}, f32[3,2048]{1,0:T(4,128)S(1)}, u32[]{:S(2)}, u32[]{:S(2)}) collective-permute-start(f32[3,2048]{1,0:T(4,128)S(1)} %pad_maximum_fusion.4), channel_id=1, source_target_pairs={{4,0},{8,4},{12,8},{16,12},{20,16},{24,20},{28,24},{32,28},{36,32}... | collective-permute-start | bytes 73736 | tf_op jit(solution)/shard_map/ppermute | solution.py:17
  50.5 1.9 copy-start.5
  50.5 7.7 collective-permute-start
  105.1 9.6 %collective-permute-start.2 = (f32[32,2048]{1,0:T(8,128)S(1)}, f32[32,2048]{1,0:T(8,128)S(1)}, u32[]{:S(2)}, u32[]{:S(2)}) collective-permute-start(f32[32,2048]{1,0:T(8,128)S(1)} %slice.81), channel_id=1, source_target_pairs={{0,4},{4,8},{8,12},{12,16},{16,20},{20,24},{24,28},{28,32},{32,36}... | collective-permute-start | bytes 786440 | tf_op jit(solution)/shard_map/ppermute | solution.py:17
  115.5 405.9 %all-reduce.7.cloned.1.call-start = ((), (), s32[]{:S(2)}) async-start(), calls=%async_computation.1 | async-start | bytes 524288 | tf_op jit(solution)/shard_map/psum | solution.py:110
  363.2 7.7 collective-permute-start.3
  417.9 10.3 %collective-permute-start.4 = (f32[32,2048]{1,0:T(8,128)S(1)}, f32[32,2048]{1,0:T(8,128)S(1)}, u32[]{:S(2)}, u32[]{:S(2)}) collective-permute-start(f32[32,2048]{1,0:T(8,128)S(1)} %slice.83), channel_id=1, source_target_pairs={{0,4},{4,8},{8,12},{12,16},{16,20},{20,24},{24,28},{28,32},{32,36}... | collective-permute-start | bytes 786440 | tf_op jit(solution)/shard_map/ppermute | solution.py:17
  428.9 403.9 %all-reduce.9.cloned.1.call-start = ((), (), s32[]{:S(2)}) async-start(), calls=%async_computation.2 | async-start | bytes 524288 | tf_op jit(solution)/shard_map/psum | solution.py:110
  674.5 7.7 collective-permute-start.5
  729.2 10.3 %collective-permute-start.6 = (f32[32,2048]{1,0:T(8,128)S(1)}, f32[32,2048]{1,0:T(8,128)S(1)}, u32[]{:S(2)}, u32[]{:S(2)}) collective-permute-start(f32[32,2048]{1,0:T(8,128)S(1)} %slice.85), channel_id=1, source_target_pairs={{0,4},{4,8},{8,12},{12,16},{16,20},{20,24},{24,28},{28,32},{32,36}... | collective-permute-start | bytes 786440 | tf_op jit(solution)/shard_map/ppermute | solution.py:17
Sparse Core Ops, SparseCore 0:
  115.6 94.4 all-reduce.4
  429.0 92.3 all-reduce.6
  740.4 92.3 all-reduce.8
where the time goes:
time: 924 us; the launch traced here: 919 us
  blocking collectives  381 us (41%)
  waiting for transfers between devices  320 us (35%)
  loops' own time  83.1 us (9%)
  local copies, waits for them, and re-layouts  70 us (8%)
  matrix products  25.3 us (3%)
  starting transfers between devices  18.1 us (2%)
  between operations  14.1 us (2%)
    psum x3, waiting for transfers between devices, local(): image = lax.psum(partial_terms, 'rep') + damping[None, :] * direction  280 us
    psum x3, blocking collectives, squares(): return lax.psum(local_sum(residual, residual), ('sites', 'rep'))  225 us
    psum x2, blocking collectives, local(): alpha = norm_now / lax.psum(local_sum(direction, image), ('sites', 'rep'))  156 us
    another operation x3, loops' own time, local(): lax.fori_loop(0, pair_total, add_pair, jnp.zeros((widened.shape[0], 2 * g...  83.1 us
    ppermute x7, waiting for transfers between devices, passed_along(): return lax.ppermute(array, axis, pairs)  40.3 us
  transfers between devices with their start and end apart: 10, of which 9 were waited for; matrix products, arithmetic and copies ran while one was open for 1% of the time, Pallas kernels for 0%

commit v1 on v0

v1 whole, which is shorter than its diff:
```python
import functools

import jax
import jax.numpy as jnp
from jax import lax
from jax.experimental import pallas as pl
from jax.experimental.pallas import tpu as pltpu
from jax.sharding import PartitionSpec as P

MESH = pl.DeviceIdType.MESH
RANGE_KM = 200.0
TAPER_UNIT = 4.0 / RANGE_KM**5
F32 = jnp.float32
BF16 = jnp.bfloat16
REACH = 4
SLOTS = 2 * REACH + 1
OFFSETS = (1, -1, 2, -2, 3, -3, 4, -4)


def split3(value):
    high = value.astype(BF16).astype(F32)
    rest = value - high
    middle = rest.astype(BF16).astype(F32)
    return high, middle, rest - middle


def kernel(
    sizes,
    coords, scale, nugget, right_side, order,
    out_solution, out_residual,
    data, tile_high, tile_low, geo, halo, last, acc, sums1, sums2,
    geo_send, geo_recv, halo_send, halo_recv, last_send, last_recv,
    sum1_send, sum1_recv, sum2_send, sum2_recv,
):
    sites_n, rep_n, z_n, y_n = sizes
    group_width = right_side.shape[1]
    months = right_side.shape[0]
    width = group_width // rep_n
    chain_n = sites_n * rep_n
    my_s = lax.axis_index("sites")
    my_r = lax.axis_index("rep")
    chain = my_s * rep_n + my_r
    my_core = my_s % 2
    my_y = (my_s // 2) % y_n
    my_z = my_s // (2 * y_n)
    n1 = rep_n * y_n
    n2 = 2 * z_n
    place1 = my_r * y_n + my_y
    place2 = my_z * 2 + my_core

    def chain_device(offset):
        other = (chain + offset + chain_n) % chain_n
        return (other // rep_n, other % rep_n)

    def device1(step):
        other = (place1 + step) % n1
        return ((my_z * y_n + other % y_n) * 2 + my_core, other // y_n)

    def device2(step):
        other = (place2 + step) % n2
        return (((other // 2) * y_n + my_y) * 2 + other % 2, my_r)

    barrier = pltpu.get_barrier_semaphore()
    peers = (
        [chain_device(offset) for offset in OFFSETS]
        + [device1(step) for step in range(1, n1)]
        + [device2(step) for step in range(1, n2)]
    )
    for peer in peers:
        pl.semaphore_signal(barrier, inc=1, device_id=peer, device_id_type=MESH)

    site = jnp.concatenate(
        [coords[...], scale[...], nugget[...], jnp.zeros((4, group_width), F32)], axis=0
    )
    for at, part in enumerate(split3(right_side[...])):
        data[at * months:(at + 1) * months, :] = part.astype(BF16)
    parts = split3(site)
    top = 3 * months
    data[top:top + 16, :] = jnp.concatenate(parts[:2], axis=0).astype(BF16)
    data[top + 16:top + 32, :] = jnp.concatenate(
        [parts[2], jnp.zeros((8, group_width), F32)], axis=0
    ).astype(BF16)
    wanted = order[:, pl.ds(pl.multiple_of(my_r * width, width), width)] - my_s * group_width
    step_rows = 256
    rows_at = lax.broadcasted_iota(jnp.int32, (step_rows, width), 0)
    placed = jnp.zeros((top + 32, width), F32)
    for at in range(group_width // step_rows):
        chosen = jnp.where(rows_at == wanted - at * step_rows, 1.0, 0.0).astype(BF16)
        placed = placed + jnp.dot(
            data[:, at * step_rows:(at + 1) * step_rows], chosen, preferred_element_type=F32
        )
    ordered = (placed[:months] + placed[months:2 * months]) + placed[2 * months:top]
    own_geo = (placed[top:top + 8] + placed[top + 8:top + 16]) + placed[top + 16:top + 24]
    geo[REACH] = own_geo
    halo[0, REACH] = ordered

    pl.semaphore_wait(barrier, len(peers))

    def spread(source_of, send_sem, recv_of):
        for offset in OFFSETS:
            pltpu.make_async_remote_copy(
                src_ref=source_of(REACH), dst_ref=source_of(REACH - offset),
                send_sem=send_sem, recv_sem=recv_of(REACH - offset),
                device_id=chain_device(offset), device_id_type=MESH,
            ).start()

    def await_bytes(ref, sem):
        pltpu.make_async_copy(ref, ref, sem).wait()

    def spread_halo(stage):
        spread(lambda slot: halo.at[stage, slot], halo_send.at[stage], lambda slot: halo_recv.at[stage, slot])

    spread(lambda slot: geo.at[slot], geo_send, lambda slot: geo_recv.at[slot])
    spread_halo(0)

    own_scale = own_geo[2:3] * TAPER_UNIT
    own_nugget = own_geo[3:4]

    def make_tiles(slot):
        away = (chain + slot - REACH < 0) | (chain + slot - REACH >= chain_n)
        shift = jnp.where(away, 1.0e6, 0.0).astype(F32)
        columns = jnp.transpose(geo[slot])
        for at in range(0, width, step_rows):
            east = columns[at:at + step_rows, 0:1] + shift
            north = columns[at:at + step_rows, 1:2]
            d_east = east - own_geo[0:1]
            d_north = north - own_geo[1:2]
            squared = jnp.clip(d_east * d_east + d_north * d_north, 1.0e-30, RANGE_KM * RANGE_KM)
            distance = squared * lax.rsqrt(squared)
            remain = RANGE_KM - distance
            square = remain * remain
            tile = (square * square) * (distance + 0.25 * RANGE_KM)
            high = tile.astype(BF16)
            tile_high[slot, at:at + step_rows, :] = high
            tile_low[slot, at:at + step_rows, :] = (tile - high.astype(F32)).astype(BF16)

    def add_product(stage, slot):
        vector = halo[stage, slot] * geo[slot][2:3]
        high = vector.astype(BF16)
        low = (vector - high.astype(F32)).astype(BF16)
        both = jnp.dot(jnp.concatenate([high, low], axis=0), tile_high[slot], preferred_element_type=F32)
        small = jnp.dot(high, tile_low[slot], preferred_element_type=F32)
        acc[...] += both[:months] + (both[months:] + small)

    def slot_of(step):
        return REACH + (1 - 2 * (step % 2)) * ((step + 1) // 2) * -1

    def product(stage, midway, first):
        acc[...] = jnp.zeros_like(acc)
        if first:
            make_tiles(REACH)
        add_product(stage, REACH)

        def one(step, carry):
            slot = slot_of(step)
            if first:
                await_bytes(geo.at[slot], geo_recv.at[slot])
                make_tiles(slot)
            await_bytes(halo.at[stage, slot], halo_recv.at[stage, slot])
            add_product(stage, slot)
            return carry

        half = 5
        lax.fori_loop(1, half, one, 0)
        midway()
        lax.fori_loop(half, SLOTS, one, 0)
        return own_scale * acc[...] + own_nugget * halo[stage, REACH]

    def begin_sum(which, first, second):
        both = jnp.concatenate([first, second], axis=0)
        folded = both[:, :128]
        for at in range(128, width, 128):
            folded = folded + both[:, at:at + 128]
        folded = jnp.concatenate([folded, jnp.zeros((128 - 2 * months, 128), F32)], axis=0)
        sums1[which, place1] = jnp.sum(jnp.transpose(folded), axis=0, keepdims=True)
        for step in range(1, n1):
            pltpu.make_async_remote_copy(
                src_ref=sums1.at[which, place1], dst_ref=sums1.at[which, place1],
                send_sem=sum1_send.at[which], recv_sem=sum1_recv.at[which],
                device_id=device1(step), device_id_type=MESH,
            ).start()

    def pass_sum(which):
        await_bytes(sums1.at[which, pl.ds(0, n1 - 1)], sum1_recv.at[which])
        sums2[which, place2] = jnp.sum(sums1[which], axis=0)
        for step in range(1, n2):
            pltpu.make_async_remote_copy(
                src_ref=sums2.at[which, place2], dst_ref=sums2.at[which, place2],
                send_sem=sum2_send.at[which], recv_sem=sum2_recv.at[which],
                device_id=device2(step), device_id_type=MESH,
            ).start()

    def end_sum(which):
        await_bytes(sums2.at[which, pl.ds(0, n2 - 1)], sum2_recv.at[which])
        total = jnp.transpose(jnp.broadcast_to(jnp.sum(sums2[which], axis=0), (8, 128)))
        return total[:months, 0:1], total[months:2 * months, 0:1]

    image = product(0, lambda: None, True)
    halo[1, REACH] = image
    spread_halo(1)
    begin_sum(0, ordered * ordered, image * ordered)
    twice = product(1, lambda: pass_sum(0), False)
    norm0, curve0 = end_sum(0)
    alpha0 = norm0 / curve0
    residual1 = halo[0, REACH] - alpha0 * halo[1, REACH]
    image1 = halo[1, REACH] - alpha0 * twice
    halo[2, REACH] = image1
    spread_halo(2)
    begin_sum(1, residual1 * residual1, image1 * residual1)
    twice1 = product(2, lambda: pass_sum(1), False)
    last[my_r] = twice1
    for step in range(1, rep_n):
        pltpu.make_async_remote_copy(
            src_ref=last.at[my_r], dst_ref=last.at[my_r],
            send_sem=last_send, recv_sem=last_recv.at[step],
            device_id=(my_s, (my_r + step) % rep_n), device_id_type=MESH,
        ).start()
    norm1, curve1 = end_sum(1)
    beta1 = norm1 / norm0
    alpha1 = norm1 / (curve1 - beta1 * norm1 / alpha0)

    def second_step(place):
        slot = REACH + place - my_r
        start, first, second = halo[0, slot], halo[1, slot], halo[2, slot]
        before = start - alpha0 * first
        moved = second + beta1 * first
        direction = before + beta1 * start
        return (
            alpha0 * start + alpha1 * direction, before - alpha1 * moved, direction, moved,
            second - alpha1 * (last[place] + beta1 * ((first - second) / alpha0)),
        )

    _, residual2, _, _, image2 = second_step(my_r)
    begin_sum(2, residual2 * residual2, image2 * residual2)
    pass_sum(2)
    norm2, curve2 = end_sum(2)
    beta2 = norm2 / norm1
    alpha2 = norm2 / (curve2 - beta2 * norm2 / alpha1)
    for step in range(1, rep_n):
        await_bytes(last.at[0], last_recv.at[step])
    for place in range(rep_n):
        at = place * width
        found, residual, direction, moved, image2 = second_step(place)
        out_solution[:, at:at + width] = found + alpha2 * (residual + beta2 * direction)
        out_residual[:, at:at + width] = residual - alpha2 * (image2 + beta2 * moved)

    count = len(OFFSETS)
    await_bytes(geo.at[pl.ds(0, count)], geo_send)
    for stage in range(3):
        await_bytes(halo.at[stage, pl.ds(0, count)], halo_send.at[stage])
        await_bytes(sums1.at[stage, pl.ds(0, n1 - 1)], sum1_send.at[stage])
        await_bytes(sums2.at[stage, pl.ds(0, n2 - 1)], sum2_send.at[stage])
    await_bytes(last.at[pl.ds(0, rep_n - 1)], last_send)


def solution(mesh):
    sites_n, rep_n = mesh.shape["sites"], mesh.shape["rep"]
    y_n = 4
    z_n = sites_n // (2 * y_n)

    def local(coords, scale, nugget, right_side, site_order, pair_list, pair_count):
        months, group_width = right_side.shape
        width = group_width // rep_n
        vmem = pl.BlockSpec(memory_space=pltpu.VMEM)
        out = jax.ShapeDtypeStruct((months, group_width), F32)
        dma = pltpu.SemaphoreType.DMA
        return pl.pallas_call(
            functools.partial(kernel, (sites_n, rep_n, z_n, y_n)),
            out_shape=(out, out),
            in_specs=[vmem] * 5,
            out_specs=(vmem, vmem),
            scratch_shapes=[
                pltpu.VMEM((3 * months + 32, group_width), BF16),
                pltpu.VMEM((SLOTS, width, width), BF16),
                pltpu.VMEM((SLOTS, width, width), BF16),
                pltpu.VMEM((SLOTS, 8, width), F32),
                pltpu.VMEM((3, SLOTS, months, width), F32),
                pltpu.VMEM((rep_n, months, width), F32),
                pltpu.VMEM((months, width), F32),
                pltpu.VMEM((3, rep_n * y_n, 1, 128), F32),
                pltpu.VMEM((3, 2 * z_n, 1, 128), F32),
                dma, dma((SLOTS,)), dma((3,)), dma((3, SLOTS)), dma, dma((rep_n,)),
                dma((3,)), dma((3,)), dma((3,)), dma((3,)),
            ],
            compiler_params=pltpu.CompilerParams(
                collective_id=0, has_side_effects=True, vmem_limit_bytes=48 * 2**20
            ),
        )(coords, scale[None, :], nugget[None, :], right_side, site_order[None, :])

    in_specs = (
        P(None, "sites"),
        P("sites"),
        P("sites"),
        P(None, "sites"),
        P("sites"),
        P(None, ("sites", "rep")),
        P(("sites", "rep")),
    )
    out_specs = (P(None, "sites"), P(None, "sites"))
    return jax.shard_map(local, mesh=mesh, in_specs=in_specs, out_specs=out_specs, check_vma=False)
```

time: 924 us -> 69.6 us (0.08)
  blocking collectives: 381 us -> 0 us
  waiting for transfers between devices: 320 us -> 0 us
  loops' own time: 83.1 us -> 0 us
  local copies, waits for them, and re-layouts: 70 us -> 5.16 us
  Pallas kernels: 0 us -> 63.4 us
  matrix products: 25.3 us -> 0 us
  starting transfers between devices: 18.1 us -> 0 us
  between operations: 14.1 us -> 0.65 us
    psum x5 -> x0, blocking collectives: 381 us -> none  [the longest x3 225 us: squares(): return lax.psum(local_sum(residual, residual), ('sites', 'rep'))]
    psum x3 -> x0, waiting for transfers between devices: 280 us -> none  [local(): image = lax.psum(partial_terms, 'rep') + damping[None, :] * direction]
    another operation x3 -> x0, loops' own time: 83.1 us -> none  [local(): lax.fori_loop(0, pair_total, add_pair, jnp.zeros((widened.shape[0], 2 * g...]
    pallas_call x0 -> x1, Pallas kernels: none -> 63.4 us  [local(): pl.pallas_call(functools.partial(kernel, (sites_n, rep_n, z_n, y_n)), out...]
    ppermute x7 -> x0, waiting for transfers between devices: 40.3 us -> none  [passed_along(): return lax.ppermute(array, axis, pairs)]
    gather x5 -> x0, local copies, waits for them, and re-layouts: 34.8 us -> none  [the longest x1 11.8 us: local(): damping = jnp.take(nugget, local_index)]
    dynamic_slice x48 -> x0, local copies, waits for them, and re-layouts: 30.1 us -> none  [the longest x24 16 us: add_pair(): col_block = col_blocks[slot_step]]
    dot_general x48 -> x0, matrix products: 25.3 us -> none  [the longest x24 13.5 us: tile_terms(): lax.dot_general(lax.dynamic_slice_in_dim(vectors, col_start, BLK, 1), til...]
  transfers between devices with their start and end apart: 10 -> 0, of which waited for: 9 -> 0; matrix products, arithmetic and copies ran while one was open for 1% -> 0% of each run, Pallas kernels for 0% -> 0%
where the time goes in v1:
time: 69.6 us; the launch traced here: 69.2 us
  Pallas kernels  63.4 us (91%)
  local copies, waits for them, and re-layouts  5.16 us (7%)
    pallas_call x1, Pallas kernels, local(): pl.pallas_call(functools.partial(kernel, (sites_n, rep_n, z_n, y_n)), out...  63.4 us
    unnamed x12, local copies, waits for them, and re-layouts  5.16 us

profile of v1, /device:TPU:1, one launch (start us, length us, event | category | flops | bytes accessed | tf_op | source)
XLA Modules:
  0.0 69.2 jit_solution(16186843785089875821)
XLA Ops:
  0.6 0.0 copy-start
  0.6 0.9 %copy-done = f32[32,2048]{1,0:T(8,128)S(1)} copy-done((f32[32,2048]{1,0:T(8,128)S(1)}, f32[32,2048]{1,0:T(8,128)}, u32[]{:S(2)}) %copy-start) | copy-done | bytes 262168
  1.6 0.0 copy-start.1
  1.6 0.7 %copy-done.1 = f32[2,2048]{1,0:T(2,128)S(1)} copy-done((f32[2,2048]{1,0:T(2,128)S(1)}, f32[2,2048]{1,0:T(2,128)}, u32[]{:S(2)}) %copy-start.1) | copy-done | bytes 16408
  2.3 0.0 copy-start.2
  2.3 0.7 %copy-done.2 = f32[2048]{0:T(1024)S(1)} copy-done((f32[2048]{0:T(1024)S(1)}, f32[2048]{0:T(1024)}, u32[]{:S(2)}) %copy-start.2) | copy-done | bytes 8216
  3.0 0.0 copy-start.3
  3.0 0.7 %copy-done.3 = f32[2048]{0:T(1024)S(1)} copy-done((f32[2048]{0:T(1024)S(1)}, f32[2048]{0:T(1024)}, u32[]{:S(2)}) %copy-start.3) | copy-done | bytes 8216
  3.7 0.0 copy-start.4
  3.7 0.7 %copy-done.4 = s32[2048]{0:T(1024)S(1)} copy-done((s32[2048]{0:T(1024)S(1)}, s32[2048]{0:T(1024)}, u32[]{:S(2)}) %copy-start.4) | copy-done | bytes 8216
  4.4 63.4 %shard_map.68 = (f32[32,2048]{1,0:T(8,128)S(1)}, f32[32,2048]{1,0:T(8,128)S(1)}) custom-call(f32[2,2048]{1,0:T(2,128)S(1)} %copy-done.1, f32[1,2048]{1,0:T(1,128)S(1)} %bitcast.3, f32[1,2048]{1,0:T(1,128)S(1)} %bitcast.4, f32[32,2048]{1,0:T(8,128)S(1)} %copy-done, s32[1,2048]{1,0:T(1,128)S(1)} %bitcast.5), custom_call_target="tpu_custom_call" | custom-call | tf_op jit(solution)/shard_map/pallas_call | solution.py:267
  67.8 0.7 %copy.9 = f32[32,2048]{1,0:T(8,128)} copy(f32[32,2048]{1,0:T(8,128)S(1)} %get-tuple-element.4) | data formatting | bytes 524288
  68.5 0.7 %copy.10 = f32[32,2048]{1,0:T(8,128)} copy(f32[32,2048]{1,0:T(8,128)S(1)} %get-tuple-element.5) | data formatting | bytes 524288
Async XLA Ops:
  0.6 1.0 %copy-start = (f32[32,2048]{1,0:T(8,128)S(1)}, f32[32,2048]{1,0:T(8,128)}, u32[]{:S(2)}) copy-start(f32[32,2048]{1,0:T(8,128)} %right_side.1) | copy-start | bytes 786436
  1.6 0.7 %copy-start.1 = (f32[2,2048]{1,0:T(2,128)S(1)}, f32[2,2048]{1,0:T(2,128)}, u32[]{:S(2)}) copy-start(f32[2,2048]{1,0:T(2,128)} %coords.1) | copy-start | bytes 49156
  2.3 0.7 %copy-start.2 = (f32[2048]{0:T(1024)S(1)}, f32[2048]{0:T(1024)}, u32[]{:S(2)}) copy-start(f32[2048]{0:T(1024)} %param.8) | copy-start | bytes 24580
  3.0 0.7 %copy-start.3 = (f32[2048]{0:T(1024)S(1)}, f32[2048]{0:T(1024)}, u32[]{:S(2)}) copy-start(f32[2048]{0:T(1024)} %param.9) | copy-start | bytes 24580
  3.7 0.7 %copy-start.4 = (s32[2048]{0:T(1024)S(1)}, s32[2048]{0:T(1024)}, u32[]{:S(2)}) copy-start(s32[2048]{0:T(1024)} %param.11) | copy-start | bytes 24580

commit v2 on v1

v2 whole, which is shorter than its diff:
```python
import functools

import jax
import jax.numpy as jnp
from jax import lax
from jax.experimental import pallas as pl
from jax.experimental.pallas import tpu as pltpu
from jax.sharding import PartitionSpec as P

MESH = pl.DeviceIdType.MESH
RANGE_KM = 200.0
TAPER_UNIT = 4.0 / RANGE_KM**5
F32 = jnp.float32
BF16 = jnp.bfloat16
REACH = 4
SLOTS = 2 * REACH + 1
OFFSETS = (2, -2, 3, -3, 1, -1, 4, -4)


def split3(value):
    high = value.astype(BF16).astype(F32)
    rest = value - high
    middle = rest.astype(BF16).astype(F32)
    return high, middle, rest - middle


def kernel(
    sizes,
    coords_in, scale_in, nugget_in, right_side_in, order_in,
    out_powers, out_factors,
    coords, scale, nugget, right_side, order,
    data, tile_high, tile_low, geo, halo, last, acc, sums1, sums2,
    in_sems, out_sem, geo_send, geo_recv, halo_send, halo_recv, last_send, last_recv,
    sum1_send, sum1_recv, sum2_send, sum2_recv,
):
    sites_n, rep_n, z_n, y_n = sizes
    months, group_width = right_side.shape
    width = group_width // rep_n
    chain_n = sites_n * rep_n
    my_s = lax.axis_index("sites")
    my_r = lax.axis_index("rep")
    chain = my_s * rep_n + my_r
    my_core = my_s % 2
    my_y = (my_s // 2) % y_n
    my_z = my_s // (2 * y_n)
    n1 = rep_n * y_n
    n2 = 2 * z_n
    place1 = my_r * y_n + my_y
    place2 = my_z * 2 + my_core

    def chain_device(offset):
        other = (chain + offset + chain_n) % chain_n
        return (other // rep_n, other % rep_n)

    def device1(step):
        other = (place1 + step) % n1
        return ((my_z * y_n + other % y_n) * 2 + my_core, other // y_n)

    def device2(step):
        other = (place2 + step) % n2
        return (((other // 2) * y_n + my_y) * 2 + other % 2, my_r)

    barrier = pltpu.get_barrier_semaphore()
    peers = (
        [device2(step) for step in range(1, n2)]
        + [device1(step) for step in range(1, n1)]
        + [chain_device(offset) for offset in OFFSETS]
    )
    for peer in peers:
        pl.semaphore_signal(barrier, inc=1, device_id=peer, device_id_type=MESH)

    loads = [
        pltpu.make_async_copy(source, target, in_sems.at[at])
        for at, (source, target) in enumerate((
            (right_side_in, right_side), (coords_in, coords), (scale_in, scale),
            (nugget_in, nugget), (order_in, order),
        ))
    ]
    for load in loads:
        load.start()
    for load in loads:
        load.wait()

    def await_bytes(ref, sem):
        pltpu.make_async_copy(ref, ref, sem).wait()

    site = jnp.concatenate(
        [coords[...], scale[...], nugget[...], jnp.zeros((4, group_width), F32)], axis=0
    )
    for at, part in enumerate(split3(right_side[...])):
        data[at * months:(at + 1) * months, :] = part.astype(BF16)
    parts = split3(site)
    top = 3 * months
    data[top:top + 16, :] = jnp.concatenate(parts[:2], axis=0).astype(BF16)
    data[top + 16:top + 32, :] = jnp.concatenate(
        [parts[2], jnp.zeros((8, group_width), F32)], axis=0
    ).astype(BF16)
    step_rows = 256
    rows_at = lax.broadcasted_iota(jnp.int32, (step_rows, width), 0)

    def own_group_slot(turn):
        return REACH - my_r + (my_r + turn) % rep_n

    def place_sites(turn, carry):
        slot = own_group_slot(turn)
        start = pl.multiple_of(((my_r + turn) % rep_n) * width, width)
        wanted = order[:, pl.ds(start, width)] - my_s * group_width
        placed = jnp.zeros((top + 32, width), F32)
        for at in range(group_width // step_rows):
            chosen = jnp.where(rows_at == wanted - at * step_rows, 1.0, 0.0).astype(BF16)
            placed = placed + jnp.dot(
                data[:, at * step_rows:(at + 1) * step_rows], chosen, preferred_element_type=F32
            )
        halo[0, slot] = (placed[:months] + placed[months:2 * months]) + placed[2 * months:top]
        geo[slot] = (placed[top:top + 8] + placed[top + 8:top + 16]) + placed[top + 16:top + 24]
        return carry

    lax.fori_loop(0, rep_n, place_sites, 0)
    own_geo = geo[REACH]
    own_scale = own_geo[2:3] * TAPER_UNIT
    own_nugget = own_geo[3:4]

    def make_tiles(slot):
        away = (chain + slot - REACH < 0) | (chain + slot - REACH >= chain_n)
        shift = jnp.where(away, 1.0e6, 0.0).astype(F32)
        columns = jnp.transpose(geo[slot])
        for at in range(0, width, step_rows):
            east = columns[at:at + step_rows, 0:1] + shift
            north = columns[at:at + step_rows, 1:2]
            d_east = east - own_geo[0:1]
            d_north = north - own_geo[1:2]
            squared = jnp.clip(d_east * d_east + d_north * d_north, 1.0e-30, RANGE_KM * RANGE_KM)
            distance = squared * lax.rsqrt(squared)
            remain = RANGE_KM - distance
            square = remain * remain
            tile = (square * square) * (distance + 0.25 * RANGE_KM)
            high = tile.astype(BF16)
            tile_high[slot, at:at + step_rows, :] = high
            tile_low[slot, at:at + step_rows, :] = (tile - high.astype(F32)).astype(BF16)

    def add_product(stage, slot):
        vector = halo[stage, slot] * geo[slot][2:3]
        high = vector.astype(BF16)
        low = (vector - high.astype(F32)).astype(BF16)
        both = jnp.dot(jnp.concatenate([high, low], axis=0), tile_high[slot], preferred_element_type=F32)
        small = jnp.dot(high, tile_low[slot], preferred_element_type=F32)
        acc[...] += both[:months] + (both[months:] + small)

    def image_of(stage):
        return own_scale * acc[...] + own_nugget * halo[stage, REACH]

    acc[...] = jnp.zeros_like(acc)

    def own_tiles(turn, carry):
        make_tiles(own_group_slot(turn))
        return carry

    lax.fori_loop(0, rep_n, own_tiles, 0)

    pl.semaphore_wait(barrier, len(peers))

    def upward(turn):
        return turn <= rep_n - 1 - my_r

    def exchange(ref_of, send_sem, recv_of):
        for turn in range(rep_n + 1):
            up = upward(turn)
            source = jnp.where(up, REACH + turn, turn)
            target = jnp.where(up, turn, REACH + turn)
            group = (my_s + jnp.where(up, 1, sites_n - 1)) % sites_n
            pltpu.make_async_remote_copy(
                src_ref=ref_of(source), dst_ref=ref_of(target), send_sem=send_sem, recv_sem=recv_of(target),
                device_id=(group, my_r), device_id_type=MESH,
            ).start()

    exchange(lambda slot: geo.at[slot], geo_send, lambda slot: geo_recv.at[slot])
    exchange(lambda slot: halo.at[0, slot], halo_send.at[0], lambda slot: halo_recv.at[0, slot])

    def own_products(turn, carry):
        add_product(0, own_group_slot(turn))
        return carry

    lax.fori_loop(0, rep_n, own_products, 0)

    def come_slot(turn):
        return jnp.where(upward(turn), turn, REACH + turn)

    def other_tiles(turn, carry):
        slot = come_slot(turn)
        await_bytes(geo.at[slot], geo_recv.at[slot])
        make_tiles(slot)
        return carry

    lax.fori_loop(0, rep_n + 1, other_tiles, 0)

    def other_products(turn, carry):
        slot = come_slot(turn)
        await_bytes(halo.at[0, slot], halo_recv.at[0, slot])
        add_product(0, slot)
        return carry

    lax.fori_loop(0, rep_n + 1, other_products, 0)

    def spread_halo(stage):
        for offset in OFFSETS:
            pltpu.make_async_remote_copy(
                src_ref=halo.at[stage, REACH], dst_ref=halo.at[stage, REACH - offset],
                send_sem=halo_send.at[stage], recv_sem=halo_recv.at[stage, REACH - offset],
                device_id=chain_device(offset), device_id_type=MESH,
            ).start()

    def write_power(power, source_of):
        for place in range(rep_n):
            pltpu.make_async_copy(
                source_of(place), out_powers.at[power, :, place * width:(place + 1) * width], out_sem
            ).start()

    def write_halo(stage):
        write_power(stage, lambda place: halo.at[stage, REACH + place - my_r])

    def product(stage):
        acc[...] = jnp.zeros_like(acc)
        add_product(stage, REACH)

        def one(step, carry):
            reach = jnp.where(step < 2, 4, jnp.where(step < 4, 1, jnp.where(step < 6, 3, 2)))
            slot = REACH + (1 - 2 * (step % 2)) * reach
            await_bytes(halo.at[stage, slot], halo_recv.at[stage, slot])
            add_product(stage, slot)
            return carry

        lax.fori_loop(0, 2 * REACH, one, 0)
        return image_of(stage)

    def folded(first, second):
        value = first * second
        total = value[:, :128]
        for at in range(128, width, 128):
            total = total + value[:, at:at + 128]
        return total

    def as_row(pieces):
        return jnp.sum(jnp.transpose(jnp.concatenate(pieces, axis=0)), axis=0, keepdims=True)

    halo[1, REACH] = image_of(0)
    spread_halo(1)
    write_halo(0)
    halo[2, REACH] = product(1)
    spread_halo(2)
    write_halo(1)
    start, first, second = halo[0, REACH], halo[1, REACH], halo[2, REACH]
    sums1[place1, 0:1] = as_row(
        [folded(start, start), folded(start, first), folded(first, first), folded(first, second)]
    )
    square2 = folded(second, second)
    third = product(2)
    sums1[place1, 1:2] = as_row(
        [square2, folded(halo[2, REACH], third), jnp.zeros((128 - 2 * months, 128), F32)]
    )
    for step in range(1, n1):
        pltpu.make_async_remote_copy(
            src_ref=sums1.at[place1], dst_ref=sums1.at[place1], send_sem=sum1_send, recv_sem=sum1_recv,
            device_id=device1(step), device_id_type=MESH,
        ).start()
    last[my_r] = third
    for step in range(1, rep_n):
        pltpu.make_async_remote_copy(
            src_ref=last.at[my_r], dst_ref=last.at[my_r],
            send_sem=last_send, recv_sem=last_recv.at[step],
            device_id=(my_s, (my_r + step) % rep_n), device_id_type=MESH,
        ).start()
    write_halo(2)
    await_bytes(sums1.at[pl.ds(0, n1 - 1)], sum1_recv)
    sums2[place2] = jnp.sum(sums1[...], axis=0)
    for step in range(1, n2):
        pltpu.make_async_remote_copy(
            src_ref=sums2.at[place2], dst_ref=sums2.at[place2], send_sem=sum2_send, recv_sem=sum2_recv,
            device_id=device2(step), device_id_type=MESH,
        ).start()
    for step in range(1, rep_n):
        await_bytes(last.at[0], last_recv.at[step])
    write_power(3, lambda place: last.at[place])
    count = len(OFFSETS)
    await_bytes(geo.at[pl.ds(0, rep_n + 1)], geo_send)
    await_bytes(halo.at[0, pl.ds(0, rep_n + 1)], halo_send.at[0])
    for stage in range(1, 3):
        await_bytes(halo.at[stage, pl.ds(0, count)], halo_send.at[stage])
    await_bytes(last.at[pl.ds(0, rep_n - 1)], last_send)
    await_bytes(sums1.at[pl.ds(0, n1 - 1)], sum1_send)
    await_bytes(out_powers, out_sem)

    await_bytes(sums2.at[pl.ds(0, n2 - 1)], sum2_recv)
    rows = jnp.sum(sums2[...], axis=0)
    total = jnp.transpose(jnp.concatenate([rows, jnp.zeros((6, 128), F32)], axis=0))
    m0, m1, m2, m3 = [total[at * months:(at + 1) * months, 0:1] for at in range(4)]
    m4, m5 = [total[at * months:(at + 1) * months, 1:2] for at in range(2)]
    alpha0 = m0 / m1
    norm1 = m0 - 2.0 * alpha0 * m1 + alpha0 * alpha0 * m2
    lead = 1.0 + norm1 / m0
    alpha1 = norm1 / (lead * lead * m1 - 2.0 * lead * alpha0 * m2 + alpha0 * alpha0 * m3)
    r1 = -(alpha0 + alpha1 * lead)
    r2 = alpha0 * alpha1
    norm2 = m0 + 2.0 * r1 * m1 + (r1 * r1 + 2.0 * r2) * m2 + 2.0 * r1 * r2 * m3 + r2 * r2 * m4
    beta2 = norm2 / norm1
    d0 = 1.0 + beta2 * lead
    d1 = r1 - beta2 * alpha0
    alpha2 = norm2 / (
        d0 * d0 * m1 + 2.0 * d0 * d1 * m2 + (d1 * d1 + 2.0 * d0 * r2) * m3 + 2.0 * d1 * r2 * m4 + r2 * r2 * m5
    )
    factors = (
        alpha0 + alpha1 * lead + alpha2 * d0, alpha2 * d1 - alpha1 * alpha0, alpha2 * r2,
        r1 - alpha2 * d0, r2 - alpha2 * d1, -alpha2 * r2,
    )
    lanes = lax.broadcasted_iota(jnp.int32, (months, 128), 1)
    table = jnp.zeros((months, 128), F32)
    for at, factor in enumerate(factors):
        table = jnp.where(lanes == at, factor, table)
    out_factors[...] = table
    await_bytes(sums2.at[pl.ds(0, n2 - 1)], sum2_send)


def solution(mesh):
    sites_n, rep_n = mesh.shape["sites"], mesh.shape["rep"]
    y_n = 4
    z_n = sites_n // (2 * y_n)

    def local(coords, scale, nugget, right_side, site_order, pair_list, pair_count):
        months, group_width = right_side.shape
        width = group_width // rep_n
        anywhere = pl.BlockSpec(memory_space=pl.ANY)
        vmem = pl.BlockSpec(memory_space=pltpu.VMEM)
        dma = pltpu.SemaphoreType.DMA
        powers, factors = pl.pallas_call(
            functools.partial(kernel, (sites_n, rep_n, z_n, y_n)),
            out_shape=(
                jax.ShapeDtypeStruct((4, months, group_width), F32), jax.ShapeDtypeStruct((months, 128), F32)
            ),
            in_specs=[anywhere] * 5,
            out_specs=(anywhere, vmem),
            scratch_shapes=[
                pltpu.VMEM((2, group_width), F32),
                pltpu.VMEM((1, group_width), F32),
                pltpu.VMEM((1, group_width), F32),
                pltpu.VMEM((months, group_width), F32),
                pltpu.VMEM((1, group_width), jnp.int32),
                pltpu.VMEM((3 * months + 32, group_width), BF16),
                pltpu.VMEM((SLOTS, width, width), BF16),
                pltpu.VMEM((SLOTS, width, width), BF16),
                pltpu.VMEM((SLOTS, 8, width), F32),
                pltpu.VMEM((3, SLOTS, months, width), F32),
                pltpu.VMEM((rep_n, months, width), F32),
                pltpu.VMEM((months, width), F32),
                pltpu.VMEM((rep_n * y_n, 2, 128), F32),
                pltpu.VMEM((2 * z_n, 2, 128), F32),
                dma((5,)), dma, dma, dma((SLOTS,)), dma((3,)), dma((3, SLOTS)), dma, dma((rep_n,)),
                dma, dma, dma, dma,
            ],
            compiler_params=pltpu.CompilerParams(
                collective_id=0, has_side_effects=True, vmem_limit_bytes=56 * 2**20
            ),
        )(coords, scale[None, :], nugget[None, :], right_side, site_order[None, :])
        part = [factors[:, at:at + 1] for at in range(6)]
        found = part[0] * powers[0] + part[1] * powers[1] + part[2] * powers[2]
        residual = powers[0] + part[3] * powers[1] + part[4] * powers[2] + part[5] * powers[3]
        return (found, residual)

    in_specs = (
        P(None, "sites"),
        P("sites"),
        P("sites"),
        P(None, "sites"),
        P("sites"),
        P(None, ("sites", "rep")),
        P(("sites", "rep")),
    )
    out_specs = (P(None, "sites"), P(None, "sites"))
    return jax.shard_map(local, mesh=mesh, in_specs=in_specs, out_specs=out_specs, check_vma=False)
```

time: 69.6 us -> 55.7 us (0.80)
  Pallas kernels: 63.4 us -> 51.4 us
  local copies, waits for them, and re-layouts: 5.16 us -> 1.25 us
  other arithmetic: 0 us -> 2.17 us
    pallas_call x1, Pallas kernels: 63.4 us -> 51.4 us  [local(): pl.pallas_call(functools.partial(kernel, (sites_n, rep_n, z_n, y_n)), out...]
    unnamed x12 -> x0, local copies, waits for them, and re-layouts: 5.16 us -> none
    add x0 -> x1, other arithmetic: none -> 2.17 us  [local(): powers[0] + part[3] * powers[1] + part[4] * powers[2] + part[5] * powers[3]]
    slice x0 -> x1, local copies, waits for them, and re-layouts: none -> 1.25 us  [local(): part = [factors[:, at:at + 1] for at in range(6)]]
where the time goes in v2:
time: 55.7 us; the launch traced here: 55.5 us
  Pallas kernels  51.4 us (92%)
  other arithmetic  2.17 us (4%)
  local copies, waits for them, and re-layouts  1.25 us (2%)
  between operations  0.64 us (1%)
    pallas_call x1, Pallas kernels, local(): pl.pallas_call(functools.partial(kernel, (sites_n, rep_n, z_n, y_n)), out...  51.4 us
    add x1, other arithmetic, local(): powers[0] + part[3] * powers[1] + part[4] * powers[2] + part[5] * powers[3]  2.17 us
    slice x1, local copies, waits for them, and re-layouts, local(): part = [factors[:, at:at + 1] for at in range(6)]  1.25 us

profile of v2, /device:TPU:1, one launch (start us, length us, event | category | flops | bytes accessed | tf_op | source)
XLA Modules:
  0.0 55.5 jit_solution(11721272996289084021)
XLA Ops:
  0.6 51.4 %shard_map.68 = (f32[4,32,2048]{2,1,0:T(8,128)}, f32[32,128]{1,0:T(8,128)}) custom-call(f32[2,2048]{1,0:T(2,128)} %coords_in.1, f32[1,2048]{1,0:T(1,128)} %bitcast.32, f32[1,2048]{1,0:T(1,128)} %bitcast.33, f32[32,2048]{1,0:T(8,128)} %right_side_in.1, s32[1,2048]{1,0:T(1,128)} %bitcast.34), custom_call_target="tpu_custom_call" | custom-call | tf_op jit(solution)/shard_map/pallas_call | solution.py:333
  52.1 1.3 %slice_reduce_fusion.2 = (f32[32]{0:T(128)S(1)}, f32[32]{0:T(128)S(1)}, f32[32]{0:T(128)S(1)}, f32[32]{0:T(128)S(1)}, f32[32]{0:T(128)S(1)}, /*index=5*/f32[32]{0:T(128)S(1)}) fusion(f32[32,128]{1,0:T(8,128)} %get-tuple-element.4), kind=kLoop, calls=%fused_computation.13 | loop fusion | bytes 1536 | tf_op jit(solution)/shard_map/slice | solution.py:362
  53.3 2.2 %fusion = (f32[32,2048]{1,0:T(8,128)}, f32[32,2048]{1,0:T(8,128)}) fusion(f32[4,32,2048]{2,1,0:T(8,128)} %get-tuple-element.5, f32[32]{0:T(128)S(1)} %get-tuple-element.7, f32[32]{0:T(128)S(1)} %get-tuple-element.8, f32[32]{0:T(128)S(1)} %get-tuple-element.6, f32[32]{0:T(128)S(1)} %get-tuple-element.9, f32[32]{0:T(128)S(1)} %get-tuple-element.10, ...), kind=kLoop, calls=%fused_computation.1 | loop fusion | flops 720896 | bytes 1573632 | tf_op jit(solution)/shard_map/add | solution.py:364

commit v3 on v2

--- a/solution.py
+++ b/solution.py
@@ -14,7 +14,9 @@
 BF16 = jnp.bfloat16
 REACH = 4
 SLOTS = 2 * REACH + 1
-OFFSETS = (2, -2, 3, -3, 1, -1, 4, -4)
+AHEAD = (-2, -3, -1, -4)
+BEHIND = (2, 3, 1, 4)
+OFFSETS = AHEAD + BEHIND
 
 
 def split3(value):
@@ -120,11 +122,16 @@
     own_scale = own_geo[2:3] * TAPER_UNIT
     own_nugget = own_geo[3:4]
 
+    def split2(vector):
+        high = vector.astype(BF16)
+        return high, (vector - high.astype(F32)).astype(BF16)
+
     def make_tiles(slot):
         away = (chain + slot - REACH < 0) | (chain + slot - REACH >= chain_n)
         shift = jnp.where(away, 1.0e6, 0.0).astype(F32)
         columns = jnp.transpose(geo[slot])
-        for at in range(0, width, step_rows):
+
+        def chunk(at):
             east = columns[at:at + step_rows, 0:1] + shift
             north = columns[at:at + step_rows, 1:2]
             d_east = east - own_geo[0:1]
@@ -133,29 +140,22 @@
             distance = squared * lax.rsqrt(squared)
             remain = RANGE_KM - distance
             square = remain * remain
-            tile = (square * square) * (distance + 0.25 * RANGE_KM)
-            high = tile.astype(BF16)
+            high, low = split2((square * square) * (distance + 0.25 * RANGE_KM))
             tile_high[slot, at:at + step_rows, :] = high
-            tile_low[slot, at:at + step_rows, :] = (tile - high.astype(F32)).astype(BF16)
+            tile_low[slot, at:at + step_rows, :] = low
+
+        for at in range(0, width, step_rows):
+            chunk(at)
 
     def add_product(stage, slot):
         vector = halo[stage, slot] * geo[slot][2:3]
-        high = vector.astype(BF16)
-        low = (vector - high.astype(F32)).astype(BF16)
+        high, low = split2(vector)
         both = jnp.dot(jnp.concatenate([high, low], axis=0), tile_high[slot], preferred_element_type=F32)
         small = jnp.dot(high, tile_low[slot], preferred_element_type=F32)
         acc[...] += both[:months] + (both[months:] + small)
 
     def image_of(stage):
         return own_scale * acc[...] + own_nugget * halo[stage, REACH]
-
-    acc[...] = jnp.zeros_like(acc)
-
-    def own_tiles(turn, carry):
-        make_tiles(own_group_slot(turn))
-        return carry
-
-    lax.fori_loop(0, rep_n, own_tiles, 0)
 
     pl.semaphore_wait(barrier, len(peers))
 
@@ -176,30 +176,25 @@
     exchange(lambda slot: geo.at[slot], geo_send, lambda slot: geo_recv.at[slot])
     exchange(lambda slot: halo.at[0, slot], halo_send.at[0], lambda slot: halo_recv.at[0, slot])
 
-    def own_products(turn, carry):
-        add_product(0, own_group_slot(turn))
+    acc[...] = jnp.zeros_like(acc)
+
+    def own_pieces(turn, carry):
+        slot = own_group_slot(turn)
+        make_tiles(slot)
+        add_product(0, slot)
         return carry
 
-    lax.fori_loop(0, rep_n, own_products, 0)
-
-    def come_slot(turn):
-        return jnp.where(upward(turn), turn, REACH + turn)
-
-    def other_tiles(turn, carry):
-        slot = come_slot(turn)
+    lax.fori_loop(0, rep_n, own_pieces, 0)
+
+    def other_pieces(turn, carry):
+        slot = jnp.where(upward(turn), turn, REACH + turn)
         await_bytes(geo.at[slot], geo_recv.at[slot])
         make_tiles(slot)
-        return carry
-
-    lax.fori_loop(0, rep_n + 1, other_tiles, 0)
-
-    def other_products(turn, carry):
-        slot = come_slot(turn)
         await_bytes(halo.at[0, slot], halo_recv.at[0, slot])
         add_product(0, slot)
         return carry
 
-    lax.fori_loop(0, rep_n + 1, other_products, 0)
+    lax.fori_loop(0, rep_n + 1, other_pieces, 0)
 
     def spread_halo(stage):
         for offset in OFFSETS:
@@ -218,19 +213,15 @@
     def write_halo(stage):
         write_power(stage, lambda place: halo.at[stage, REACH + place - my_r])
 
-    def product(stage):
-        acc[...] = jnp.zeros_like(acc)
-        add_product(stage, REACH)
-
+    def add_side(stage, sign):
         def one(step, carry):
-            reach = jnp.where(step < 2, 4, jnp.where(step < 4, 1, jnp.where(step < 6, 3, 2)))
-            slot = REACH + (1 - 2 * (step % 2)) * reach
+            reach = jnp.where(step == 0, 4, jnp.where(step == 1, 1, jnp.where(step == 2, 3, 2)))
+            slot = REACH + sign * reach
             await_bytes(halo.at[stage, slot], halo_recv.at[stage, slot])
             add_product(stage, slot)
             return carry
 
-        lax.fori_loop(0, 2 * REACH, one, 0)
-        return image_of(stage)
+        lax.fori_loop(0, REACH, one, 0)
 
     def folded(first, second):
         value = first * second
@@ -245,7 +236,11 @@
     halo[1, REACH] = image_of(0)
     spread_halo(1)
     write_halo(0)
-    halo[2, REACH] = product(1)
+    acc[...] = jnp.zeros_like(acc)
+    add_product(1, REACH)
+    add_side(1, 1)
+    add_side(1, -1)
+    halo[2, REACH] = image_of(1)
     spread_halo(2)
     write_halo(1)
     start, first, second = halo[0, REACH], halo[1, REACH], halo[2, REACH]
@@ -253,16 +248,21 @@
         [folded(start, start), folded(start, first), folded(first, first), folded(first, second)]
     )
     square2 = folded(second, second)
-    third = product(2)
+    acc[...] = jnp.zeros_like(acc)
+    add_product(2, REACH)
+    within = acc[...]
+    add_side(2, 1)
+    doubled = own_scale * (2.0 * acc[...] - within) + own_nugget * halo[2, REACH]
     sums1[place1, 1:2] = as_row(
-        [square2, folded(halo[2, REACH], third), jnp.zeros((128 - 2 * months, 128), F32)]
+        [square2, folded(halo[2, REACH], doubled), jnp.zeros((128 - 2 * months, 128), F32)]
     )
     for step in range(1, n1):
         pltpu.make_async_remote_copy(
             src_ref=sums1.at[place1], dst_ref=sums1.at[place1], send_sem=sum1_send, recv_sem=sum1_recv,
             device_id=device1(step), device_id_type=MESH,
         ).start()
-    last[my_r] = third
+    add_side(2, -1)
+    last[my_r] = image_of(2)
     for step in range(1, rep_n):
         pltpu.make_async_remote_copy(
             src_ref=last.at[my_r], dst_ref=last.at[my_r],
@@ -295,18 +295,16 @@
     m0, m1, m2, m3 = [total[at * months:(at + 1) * months, 0:1] for at in range(4)]
     m4, m5 = [total[at * months:(at + 1) * months, 1:2] for at in range(2)]
     alpha0 = m0 / m1
-    norm1 = m0 - 2.0 * alpha0 * m1 + alpha0 * alpha0 * m2
+    norm1 = alpha0 * alpha0 * m2 - m0
     lead = 1.0 + norm1 / m0
-    alpha1 = norm1 / (lead * lead * m1 - 2.0 * lead * alpha0 * m2 + alpha0 * alpha0 * m3)
+    alpha1 = norm1 / (alpha0 * (alpha0 * m3 - lead * m2))
     r1 = -(alpha0 + alpha1 * lead)
     r2 = alpha0 * alpha1
-    norm2 = m0 + 2.0 * r1 * m1 + (r1 * r1 + 2.0 * r2) * m2 + 2.0 * r1 * r2 * m3 + r2 * r2 * m4
+    norm2 = r2 * (m2 + r1 * m3 + r2 * m4)
     beta2 = norm2 / norm1
     d0 = 1.0 + beta2 * lead
     d1 = r1 - beta2 * alpha0
-    alpha2 = norm2 / (
-        d0 * d0 * m1 + 2.0 * d0 * d1 * m2 + (d1 * d1 + 2.0 * d0 * r2) * m3 + 2.0 * d1 * r2 * m4 + r2 * r2 * m5
-    )
+    alpha2 = norm2 / (r2 * (d0 * m3 + d1 * m4 + r2 * m5))
     factors = (
         alpha0 + alpha1 * lead + alpha2 * d0, alpha2 * d1 - alpha1 * alpha0, alpha2 * r2,
         r1 - alpha2 * d0, r2 - alpha2 * d1, -alpha2 * r2,
@@ -317,6 +315,30 @@
         table = jnp.where(lanes == at, factor, table)
     out_factors[...] = table
     await_bytes(sums2.at[pl.ds(0, n2 - 1)], sum2_send)
+
+
+def combine(powers, factors, out_solution, out_residual, held, made, in_sems, out_sems):
+    parts = in_sems.shape[0]
+    width = held.shape[2] // parts
+    loads, stores = [], []
+    for at in range(parts):
+        lanes = slice(at * width, (at + 1) * width)
+        load = pltpu.make_async_copy(powers.at[:, :, lanes], held.at[:, :, lanes], in_sems.at[at])
+        load.start()
+        loads.append(load)
+    part = [factors[:, at:at + 1] for at in range(6)]
+    for at in range(parts):
+        lanes = slice(at * width, (at + 1) * width)
+        loads[at].wait()
+        start, first, second, third = (held[power, :, lanes] for power in range(4))
+        made[0, :, lanes] = part[0] * start + part[1] * first + part[2] * second
+        made[1, :, lanes] = start + part[3] * first + part[4] * second + part[5] * third
+        for which, out in enumerate((out_solution, out_residual)):
+            store = pltpu.make_async_copy(made.at[which, :, lanes], out.at[:, lanes], out_sems.at[which, at])
+            store.start()
+            stores.append(store)
+    for store in stores:
+        store.wait()
 
 
 def solution(mesh):
@@ -359,10 +381,18 @@
                 collective_id=0, has_side_effects=True, vmem_limit_bytes=56 * 2**20
             ),
         )(coords, scale[None, :], nugget[None, :], right_side, site_order[None, :])
-        part = [factors[:, at:at + 1] for at in range(6)]
-        found = part[0] * powers[0] + part[1] * powers[1] + part[2] * powers[2]
-        residual = powers[0] + part[3] * powers[1] + part[4] * powers[2] + part[5] * powers[3]
-        return (found, residual)
+        out = jax.ShapeDtypeStruct((months, group_width), F32)
+        return pl.pallas_call(
+            combine,
+            out_shape=(out, out),
+            in_specs=[anywhere, vmem],
+            out_specs=(anywhere, anywhere),
+            scratch_shapes=[
+                pltpu.VMEM((4, months, group_width), F32), pltpu.VMEM((2, months, group_width), F32),
+                dma((rep_n,)), dma((2, rep_n)),
+            ],
+            compiler_params=pltpu.CompilerParams(vmem_limit_bytes=56 * 2**20),
+        )(powers, factors)
 
     in_specs = (
         P(None, "sites"),

time: 55.7 us -> 51.2 us (0.919)
  other arithmetic: 2.17 us -> 0 us
  local copies, waits for them, and re-layouts: 1.25 us -> 0 us
  Pallas kernels: 51.4 us -> 50.4 us
    pallas_call x1, Pallas kernels: 51.4 us -> 47.7 us  [local(): pl.pallas_call(functools.partial(kernel, (sites_n, rep_n, z_n, y_n)), out...]
    pallas_call x0 -> x1, Pallas kernels: none -> 2.69 us  [local(): pl.pallas_call(combine, out_shape=(out, out), in_specs=[anywhere, vmem],...]
    add x1 -> x0, other arithmetic: 2.17 us -> none  [local(): powers[0] + part[3] * powers[1] + part[4] * powers[2] + part[5] * powers[3]]
    slice x1 -> x0, local copies, waits for them, and re-layouts: 1.25 us -> none  [local(): part = [factors[:, at:at + 1] for at in range(6)]]
where the time goes in v3:
time: 51.2 us; the launch traced here: 51 us
  Pallas kernels  50.4 us (98%)
  between operations  0.64 us (1%)
    pallas_call x1, Pallas kernels, local(): pl.pallas_call(functools.partial(kernel, (sites_n, rep_n, z_n, y_n)), out...  47.7 us
    pallas_call x1, Pallas kernels, local(): pl.pallas_call(combine, out_shape=(out, out), in_specs=[anywhere, vmem],...  2.69 us

profile of v3, /device:TPU:1, one launch (start us, length us, event | category | flops | bytes accessed | tf_op | source)
XLA Modules:
  0.0 51.0 jit_solution(14392669740778758036)
XLA Ops:
  0.6 47.7 %shard_map.68 = (f32[4,32,2048]{2,1,0:T(8,128)}, f32[32,128]{1,0:T(8,128)}) custom-call(f32[2,2048]{1,0:T(2,128)} %coords_in.1, f32[1,2048]{1,0:T(1,128)} %bitcast.3, f32[1,2048]{1,0:T(1,128)} %bitcast.4, f32[32,2048]{1,0:T(8,128)} %right_side_in.1, s32[1,2048]{1,0:T(1,128)} %bitcast.5), custom_call_target="tpu_custom_call" | custom-call | tf_op jit(solution)/shard_map/pallas_call | solution.py:355
  48.4 2.7 %shard_map.69 = (f32[32,2048]{1,0:T(8,128)}, f32[32,2048]{1,0:T(8,128)}) custom-call(f32[4,32,2048]{2,1,0:T(8,128)} %get-tuple-element.4.powers, f32[32,128]{1,0:T(8,128)} %get-tuple-element.5.factors), custom_call_target="tpu_custom_call" | custom-call | tf_op jit(solution)/shard_map/pallas_call | solution.py:385

commit v4 on v3

v4 whole, which is shorter than its diff:
```python
import functools

import jax
import jax.numpy as jnp
from jax import lax
from jax.experimental import pallas as pl
from jax.experimental.pallas import tpu as pltpu
from jax.sharding import PartitionSpec as P

MESH = pl.DeviceIdType.MESH
RANGE_KM = 200.0
TAPER_UNIT = 4.0 / RANGE_KM**5
F32 = jnp.float32
BF16 = jnp.bfloat16
REACH = 4
SLOTS = 2 * REACH + 1
AHEAD = (-2, -3, -1, -4)
BEHIND = (2, 3, 1, 4)
OFFSETS = AHEAD + BEHIND


def split3(value):
    high = value.astype(BF16).astype(F32)
    rest = value - high
    middle = rest.astype(BF16).astype(F32)
    return high, middle, rest - middle


def kernel(
    sizes,
    coords_in, scale_in, nugget_in, right_side_in, order_in,
    out_solution, out_residual,
    coords, scale, nugget, right_side, order,
    data, tile_high, tile_low, geo, halo, last, acc, sums1, sums2, late1, late2, held, made,
    in_sems, out_sem, geo_send, geo_recv, halo_send, halo_recv, last_send, last_recv,
    sum_send, sum_recv, told,
):
    sites_n, rep_n, z_n, y_n = sizes
    months, group_width = right_side.shape
    width = group_width // rep_n
    chain_n = sites_n * rep_n
    my_s = lax.axis_index("sites")
    my_r = lax.axis_index("rep")
    chain = my_s * rep_n + my_r
    my_core = my_s % 2
    my_y = (my_s // 2) % y_n
    my_z = my_s // (2 * y_n)
    n1 = rep_n * y_n
    n2 = 2 * z_n
    place1 = my_r * y_n + my_y
    place2 = my_z * 2 + my_core

    def chain_device(offset):
        other = (chain + offset + chain_n) % chain_n
        return (other // rep_n, other % rep_n)

    def device1(step):
        other = (place1 + step) % n1
        return ((my_z * y_n + other % y_n) * 2 + my_core, other // y_n)

    def device2(step):
        other = (place2 + step) % n2
        return (((other // 2) * y_n + my_y) * 2 + other % 2, my_r)

    barrier = pltpu.get_barrier_semaphore()
    peers = (
        [chain_device(REACH), chain_device(-REACH)]
        + [(my_s, (my_r + step) % rep_n) for step in range(1, rep_n)]
    )
    for peer in peers:
        pl.semaphore_signal(barrier, inc=1, device_id=peer, device_id_type=MESH)

    loads = [
        pltpu.make_async_copy(source, target, in_sems.at[at])
        for at, (source, target) in enumerate((
            (right_side_in, right_side), (coords_in, coords), (scale_in, scale),
            (nugget_in, nugget), (order_in, order),
        ))
    ]
    for load in loads:
        load.start()
    for load in loads:
        load.wait()

    def tell(step):
        for group in (my_s + 2**step, my_s + sites_n - 2**step):
            pl.semaphore_signal(
                told.at[step], inc=1, device_id=(group % sites_n, my_r), device_id_type=MESH
            )

    def hear(step):
        pl.semaphore_wait(told.at[step], 2)

    def await_bytes(ref, sem):
        pltpu.make_async_copy(ref, ref, sem).wait()

    site = jnp.concatenate(
        [coords[...], scale[...], nugget[...], jnp.zeros((4, group_width), F32)], axis=0
    )
    for at, part in enumerate(split3(right_side[...])):
        data[at * months:(at + 1) * months, :] = part.astype(BF16)
    parts = split3(site)
    top = 3 * months
    data[top:top + 16, :] = jnp.concatenate(parts[:2], axis=0).astype(BF16)
    data[top + 16:top + 32, :] = jnp.concatenate(
        [parts[2], jnp.zeros((8, group_width), F32)], axis=0
    ).astype(BF16)
    step_rows = 256
    rows_at = lax.broadcasted_iota(jnp.int32, (step_rows, width), 0)

    def own_group_slot(turn):
        return REACH - my_r + (my_r + turn) % rep_n

    def place_sites(turn, carry):
        slot = own_group_slot(turn)
        start = pl.multiple_of(((my_r + turn) % rep_n) * width, width)
        wanted = order[:, pl.ds(start, width)] - my_s * group_width
        placed = jnp.zeros((top + 32, width), F32)
        for at in range(group_width // step_rows):
            chosen = jnp.where(rows_at == wanted - at * step_rows, 1.0, 0.0).astype(BF16)
            placed = placed + jnp.dot(
                data[:, at * step_rows:(at + 1) * step_rows], chosen, preferred_element_type=F32
            )
        halo[0, slot] = (placed[:months] + placed[months:2 * months]) + placed[2 * months:top]
        geo[slot] = (placed[top:top + 8] + placed[top + 8:top + 16]) + placed[top + 16:top + 24]
        return carry

    lax.fori_loop(0, rep_n, place_sites, 0)
    own_geo = geo[REACH]
    own_scale = own_geo[2:3] * TAPER_UNIT
    own_nugget = own_geo[3:4]

    def split2(vector):
        high = vector.astype(BF16)
        return high, (vector - high.astype(F32)).astype(BF16)

    def parts_of(stage, slot):
        high, low = split2(halo[stage, slot] * geo[slot][2:3])
        return jnp.concatenate([high, low], axis=0), high

    def tile_product(both, high, tiles, rest):
        large = jnp.dot(both, tiles, preferred_element_type=F32)
        small = jnp.dot(high, rest, preferred_element_type=F32)
        return large[:months] + (large[months:] + small)

    def add_product(stage, slot):
        both, high = parts_of(stage, slot)
        acc[...] += tile_product(both, high, tile_high[slot], tile_low[slot])

    def make_tiles(slot, use, out_of_reach=None):
        away = (chain + slot - REACH < 0) | (chain + slot - REACH >= chain_n)
        shift = jnp.where(away, 1.0e6, 0.0).astype(F32)
        columns = jnp.transpose(geo[slot])
        if use:
            both, first = parts_of(0, slot)
        total = jnp.zeros((months, width), F32)
        for at in range(0, width, step_rows):
            lanes = slice(0, width)
            if out_of_reach and out_of_reach[0] == at:
                lanes = slice(0, out_of_reach[1]) if out_of_reach[1] else slice(step_rows, width)
            east = columns[at:at + step_rows, 0:1] + shift
            north = columns[at:at + step_rows, 1:2]
            d_east = east - own_geo[0:1, lanes]
            d_north = north - own_geo[1:2, lanes]
            squared = jnp.clip(d_east * d_east + d_north * d_north, 1.0e-30, RANGE_KM * RANGE_KM)
            distance = squared * lax.rsqrt(squared)
            remain = RANGE_KM - distance
            square = remain * remain
            high, low = split2((square * square) * (distance + 0.25 * RANGE_KM))
            if out_of_reach and out_of_reach[0] == at:
                blank = slice(out_of_reach[1], out_of_reach[1] + step_rows)
                tile_high[slot, at:at + step_rows, blank] = jnp.zeros((step_rows, step_rows), BF16)
                tile_low[slot, at:at + step_rows, blank] = jnp.zeros((step_rows, step_rows), BF16)
            tile_high[slot, at:at + step_rows, lanes] = high
            tile_low[slot, at:at + step_rows, lanes] = low
            if use:
                total = total + tile_product(
                    both[:, at:at + step_rows], first[:, at:at + step_rows], high, low
                )
        if use:
            acc[...] += total

    def image_of(stage):
        return own_scale * acc[...] + own_nugget * halo[stage, REACH]

    pl.semaphore_wait(barrier, len(peers))
    tell(0)

    def upward(turn):
        return turn <= rep_n - 1 - my_r

    def exchange(ref_of, send_sem, recv_of):
        for turn in range(rep_n + 1):
            up = upward(turn)
            source = jnp.where(up, REACH + turn, turn)
            target = jnp.where(up, turn, REACH + turn)
            group = (my_s + jnp.where(up, 1, sites_n - 1)) % sites_n
            pltpu.make_async_remote_copy(
                src_ref=ref_of(source), dst_ref=ref_of(target), send_sem=send_sem, recv_sem=recv_of(target),
                device_id=(group, my_r), device_id_type=MESH,
            ).start()

    exchange(lambda slot: geo.at[slot], geo_send, lambda slot: geo_recv.at[slot])
    exchange(lambda slot: halo.at[0, slot], halo_send.at[0], lambda slot: halo_recv.at[0, slot])

    acc[...] = jnp.zeros_like(acc)

    def own_pieces(turn, carry):
        make_tiles(own_group_slot(turn), True)
        return carry

    lax.fori_loop(0, rep_n, own_pieces, 0)
    hear(0)
    tell(1)

    def come_slot(turn):
        return jnp.where(upward(turn), turn, REACH + turn)

    def other_tiles(turn, carry):
        slot = come_slot(turn)
        await_bytes(geo.at[slot], geo_recv.at[slot])
        make_tiles(slot, False)
        return carry

    await_bytes(geo.at[0], geo_recv.at[0])
    make_tiles(0, False, (0, width - step_rows))
    lax.fori_loop(1, rep_n, other_tiles, 0)
    await_bytes(geo.at[2 * REACH], geo_recv.at[2 * REACH])
    make_tiles(2 * REACH, False, (width - step_rows, 0))
    hear(1)
    tell(2)
    for turn in range(rep_n + 1):
        slot = come_slot(turn)
        await_bytes(halo.at[0, slot], halo_recv.at[0, slot])
        add_product(0, slot)

    def spread_halo(stage):
        for offset in OFFSETS:
            pltpu.make_async_remote_copy(
                src_ref=halo.at[stage, REACH], dst_ref=halo.at[stage, REACH - offset],
                send_sem=halo_send.at[stage], recv_sem=halo_recv.at[stage, REACH - offset],
                device_id=chain_device(offset), device_id_type=MESH,
            ).start()

    def add_side(stage, offsets):
        for offset in offsets:
            slot = REACH - offset
            await_bytes(halo.at[stage, slot], halo_recv.at[stage, slot])
            add_product(stage, slot)

    def folded(first, second):
        value = first * second
        total = value[:, :128]
        for at in range(128, width, 128):
            total = total + value[:, at:at + 128]
        return total

    def as_row(pieces):
        return jnp.sum(jnp.transpose(jnp.concatenate(pieces, axis=0)), axis=0, keepdims=True)

    def columns_of(row):
        return jnp.transpose(jnp.concatenate([row, jnp.zeros((8 - row.shape[0], 128), F32)], axis=0))

    def begin_sum(slots, send_sem, recv_sem):
        for step in range(1, n1):
            pltpu.make_async_remote_copy(
                src_ref=slots.at[place1], dst_ref=slots.at[place1], send_sem=send_sem, recv_sem=recv_sem,
                device_id=device1(step), device_id_type=MESH,
            ).start()

    def pass_sum(slots, recv_sem, slots_next, send_sem_next, recv_sem_next):
        await_bytes(slots.at[pl.ds(0, n1 - 1)], recv_sem)
        slots_next[place2] = jnp.sum(slots[...], axis=0)
        for step in range(1, n2):
            pltpu.make_async_remote_copy(
                src_ref=slots_next.at[place2], dst_ref=slots_next.at[place2],
                send_sem=send_sem_next, recv_sem=recv_sem_next,
                device_id=device2(step), device_id_type=MESH,
            ).start()

    def end_sum(slots, recv_sem):
        await_bytes(slots.at[pl.ds(0, n2 - 1)], recv_sem)
        return columns_of(jnp.sum(slots[...], axis=0))

    halo[1, REACH] = image_of(0)
    spread_halo(1)
    acc[...] = jnp.zeros_like(acc)
    add_product(1, REACH)
    hear(2)
    tell(3)
    add_side(1, AHEAD)
    hear(3)
    tell(4)
    add_side(1, BEHIND)
    halo[2, REACH] = image_of(1)
    spread_halo(2)
    start, first, second = halo[0, REACH], halo[1, REACH], halo[2, REACH]
    sums1[place1, 0:1] = as_row(
        [folded(start, start), folded(start, first), folded(first, first), folded(first, second)]
    )
    sums1[place1, 1:2] = as_row([folded(second, second), jnp.zeros((128 - months, 128), F32)])
    begin_sum(sums1, sum_send.at[0], sum_recv.at[0])
    acc[...] = jnp.zeros_like(acc)
    add_product(2, REACH)
    within = acc[...]
    add_side(2, AHEAD)
    doubled = own_scale * (2.0 * acc[...] - within) + own_nugget * halo[2, REACH]
    late1[place1] = as_row([folded(halo[2, REACH], doubled), jnp.zeros((128 - months, 128), F32)])
    begin_sum(late1, sum_send.at[2], sum_recv.at[2])
    hear(4)
    pass_sum(sums1, sum_recv.at[0], sums2, sum_send.at[1], sum_recv.at[1])
    add_side(2, BEHIND)
    last[my_r] = image_of(2)
    for step in range(1, rep_n):
        pltpu.make_async_remote_copy(
            src_ref=last.at[my_r], dst_ref=last.at[my_r],
            send_sem=last_send, recv_sem=last_recv.at[step],
            device_id=(my_s, (my_r + step) % rep_n), device_id_type=MESH,
        ).start()
    pass_sum(late1, sum_recv.at[2], late2, sum_send.at[3], sum_recv.at[3])

    total = end_sum(sums2, sum_recv.at[1])
    m0, m1, m2, m3 = [total[at * months:(at + 1) * months, 0:1] for at in range(4)]
    m4 = total[:months, 1:2]
    alpha0 = m0 / m1
    norm1 = alpha0 * alpha0 * m2 - m0
    lead = 1.0 + norm1 / m0
    alpha1 = norm1 / (alpha0 * (alpha0 * m3 - lead * m2))
    r1 = -(alpha0 + alpha1 * lead)
    r2 = alpha0 * alpha1
    norm2 = r2 * (m2 + r1 * m3 + r2 * m4)
    beta2 = norm2 / norm1
    d0 = 1.0 + beta2 * lead
    d1 = r1 - beta2 * alpha0
    for step in range(1, rep_n):
        await_bytes(last.at[0], last_recv.at[step])
    for place in range(rep_n):
        lanes = slice(place * width, (place + 1) * width)
        slot = REACH + place - my_r
        start, first, second = halo[0, slot], halo[1, slot], halo[2, slot]
        held[0, :, lanes] = (alpha0 + alpha1 * lead) * start - (alpha1 * alpha0) * first
        held[1, :, lanes] = d0 * start + d1 * first + r2 * second
        held[2, :, lanes] = start + r1 * first + r2 * second
        held[3, :, lanes] = d0 * first + d1 * second + r2 * last[place]
    count = len(OFFSETS)
    await_bytes(geo.at[pl.ds(0, rep_n + 1)], geo_send)
    await_bytes(halo.at[0, pl.ds(0, rep_n + 1)], halo_send.at[0])
    for stage in range(1, 3):
        await_bytes(halo.at[stage, pl.ds(0, count)], halo_send.at[stage])
    await_bytes(last.at[pl.ds(0, rep_n - 1)], last_send)
    await_bytes(sums1.at[pl.ds(0, n1 - 1)], sum_send.at[0])
    await_bytes(sums2.at[pl.ds(0, n2 - 1)], sum_send.at[1])
    await_bytes(late1.at[pl.ds(0, n1 - 1)], sum_send.at[2])

    m5 = end_sum(late2, sum_recv.at[3])[:months, 0:1]
    alpha2 = norm2 / (r2 * (d0 * m3 + d1 * m4 + r2 * m5))
    stores = []
    for place in range(rep_n):
        lanes = slice(place * width, (place + 1) * width)
        made[0, :, lanes] = held[0, :, lanes] + alpha2 * held[1, :, lanes]
        made[1, :, lanes] = held[2, :, lanes] - alpha2 * held[3, :, lanes]
        for which, out in enumerate((out_solution, out_residual)):
            store = pltpu.make_async_copy(made.at[which, :, lanes], out.at[:, lanes], out_sem.at[which, place])
            store.start()
            stores.append(store)
    for store in stores:
        store.wait()
    await_bytes(late2.at[pl.ds(0, n2 - 1)], sum_send.at[3])


def solution(mesh):
    sites_n, rep_n = mesh.shape["sites"], mesh.shape["rep"]
    y_n = 4
    z_n = sites_n // (2 * y_n)

    def local(coords, scale, nugget, right_side, site_order, pair_list, pair_count):
        months, group_width = right_side.shape
        width = group_width // rep_n
        anywhere = pl.BlockSpec(memory_space=pl.ANY)
        dma = pltpu.SemaphoreType.DMA
        out = jax.ShapeDtypeStruct((months, group_width), F32)
        return pl.pallas_call(
            functools.partial(kernel, (sites_n, rep_n, z_n, y_n)),
            out_shape=(out, out),
            in_specs=[anywhere] * 5,
            out_specs=(anywhere, anywhere),
            scratch_shapes=[
                pltpu.VMEM((2, group_width), F32),
                pltpu.VMEM((1, group_width), F32),
                pltpu.VMEM((1, group_width), F32),
                pltpu.VMEM((months, group_width), F32),
                pltpu.VMEM((1, group_width), jnp.int32),
                pltpu.VMEM((3 * months + 32, group_width), BF16),
                pltpu.VMEM((SLOTS, width, width), BF16),
                pltpu.VMEM((SLOTS, width, width), BF16),
                pltpu.VMEM((SLOTS, 8, width), F32),
                pltpu.VMEM((3, SLOTS, months, width), F32),
                pltpu.VMEM((rep_n, months, width), F32),
                pltpu.VMEM((months, width), F32),
                pltpu.VMEM((rep_n * y_n, 2, 128), F32),
                pltpu.VMEM((2 * z_n, 2, 128), F32),
                pltpu.VMEM((rep_n * y_n, 1, 128), F32),
                pltpu.VMEM((2 * z_n, 1, 128), F32),
                pltpu.VMEM((4, months, group_width), F32),
                pltpu.VMEM((2, months, group_width), F32),
                dma((5,)), dma((2, rep_n)), dma, dma((SLOTS,)), dma((3,)), dma((3, SLOTS)), dma, dma((rep_n,)),
                dma((4,)), dma((4,)), pltpu.SemaphoreType.REGULAR((5,)),
            ],
            compiler_params=pltpu.CompilerParams(
                collective_id=0, has_side_effects=True, vmem_limit_bytes=56 * 2**20
            ),
        )(coords, scale[None, :], nugget[None, :], right_side, site_order[None, :])

    in_specs = (
        P(None, "sites"),
        P("sites"),
        P("sites"),
        P(None, "sites"),
        P("sites"),
        P(None, ("sites", "rep")),
        P(("sites", "rep")),
    )
    out_specs = (P(None, "sites"), P(None, "sites"))
    return jax.shard_map(local, mesh=mesh, in_specs=in_specs, out_specs=out_specs, check_vma=False)
```

time: 51.2 us -> 47.6 us (0.930)
  Pallas kernels: 50.4 us -> 44.4 us
  local copies, waits for them, and re-layouts: 0 us -> 2.42 us
    pallas_call x1, Pallas kernels: 47.7 us -> 44.4 us  [local(): pl.pallas_call(functools.partial(kernel, (sites_n, rep_n, z_n, y_n)), out...]
    pallas_call x1 -> x0, Pallas kernels: 2.69 us -> none  [local(): pl.pallas_call(combine, out_shape=(out, out), in_specs=[anywhere, vmem],...]
    unnamed x0 -> x4, local copies, waits for them, and re-layouts: none -> 2.42 us
where the time goes in v4:
time: 47.6 us; the launch traced here: 47.5 us
  Pallas kernels  44.4 us (93%)
  local copies, waits for them, and re-layouts  2.42 us (5%)
  between operations  0.65 us (1%)
    pallas_call x1, Pallas kernels, local(): pl.pallas_call(functools.partial(kernel, (sites_n, rep_n, z_n, y_n)), out...  44.4 us
    unnamed x4, local copies, waits for them, and re-layouts  2.42 us

profile of v4, /device:TPU:1, one launch (start us, length us, event | category | flops | bytes accessed | tf_op | source)
XLA Modules:
  0.0 47.5 jit_solution(4514785789706486597)
XLA Ops:
  0.6 44.4 %shard_map.68 = (f32[32,2048]{1,0:T(8,128)}, f32[32,2048]{1,0:T(8,128)}) custom-call(f32[2,2048]{1,0:T(2,128)} %coords_in.1, f32[1,2048]{1,0:T(1,128)} %bitcast.3, f32[1,2048]{1,0:T(1,128)} %bitcast.4, f32[32,2048]{1,0:T(8,128)} %right_side_in.1, s32[1,2048]{1,0:T(1,128)} %bitcast.5), custom_call_target="tpu_custom_call" | custom-call | tf_op jit(solution)/shard_map/pallas_call | solution.py:382
  45.0 0.0 copy-start
  45.0 1.7 %copy.9 = f32[32,2048]{1,0:T(8,128)} copy(f32[32,2048]{1,0:T(8,128)} %get-tuple-element.4) | data formatting | bytes 524288
  46.8 0.0 copy-done
  46.8 0.7 %copy.10 = f32[32,2048]{1,0:T(8,128)} copy(f32[32,2048]{1,0:T(8,128)S(1)} %copy-done) | data formatting | bytes 524288
Async XLA Ops:
  45.0 1.7 %copy-start = (f32[32,2048]{1,0:T(8,128)S(1)}, f32[32,2048]{1,0:T(8,128)}, u32[]{:S(2)}) copy-start(f32[32,2048]{1,0:T(8,128)} %get-tuple-element.5) | copy-start | bytes 786436

commit v5 on v4

--- a/solution.py
+++ b/solution.py
@@ -26,14 +26,18 @@
     return high, middle, rest - middle
 
 
+def swing(count):
+    return sorted(range(count), key=lambda ahead: -min(ahead, count - ahead))
+
+
 def kernel(
     sizes,
     coords_in, scale_in, nugget_in, right_side_in, order_in,
     out_solution, out_residual,
     coords, scale, nugget, right_side, order,
-    data, tile_high, tile_low, geo, halo, last, acc, sums1, sums2, late1, late2, held, made,
+    data, tile_high, tile_low, geo, halo, last, acc, sums1, sums2, late, pair, made,
     in_sems, out_sem, geo_send, geo_recv, halo_send, halo_recv, last_send, last_recv,
-    sum_send, sum_recv, told,
+    sum_send, sum_recv, pair_sems, told,
 ):
     sites_n, rep_n, z_n, y_n = sizes
     months, group_width = right_side.shape
@@ -49,6 +53,7 @@
     n2 = 2 * z_n
     place1 = my_r * y_n + my_y
     place2 = my_z * 2 + my_core
+    chip = (my_s // 2) * rep_n + my_r
 
     def chain_device(offset):
         other = (chain + offset + chain_n) % chain_n
@@ -286,29 +291,48 @@
     spread_halo(1)
     acc[...] = jnp.zeros_like(acc)
     add_product(1, REACH)
+    start, first = halo[0, REACH], halo[1, REACH]
+    sums1[place1] = as_row([
+        folded(start, start), folded(start, first), folded(first, first), jnp.zeros((128 - 3 * months, 128), F32)
+    ])
     hear(2)
     tell(3)
+    begin_sum(sums1, sum_send.at[0], sum_recv.at[0])
     add_side(1, AHEAD)
     hear(3)
     tell(4)
     add_side(1, BEHIND)
     halo[2, REACH] = image_of(1)
     spread_halo(2)
-    start, first, second = halo[0, REACH], halo[1, REACH], halo[2, REACH]
-    sums1[place1, 0:1] = as_row(
-        [folded(start, start), folded(start, first), folded(first, first), folded(first, second)]
-    )
-    sums1[place1, 1:2] = as_row([folded(second, second), jnp.zeros((128 - months, 128), F32)])
-    begin_sum(sums1, sum_send.at[0], sum_recv.at[0])
+    hear(4)
+    pass_sum(sums1, sum_recv.at[0], sums2, sum_send.at[1], sum_recv.at[1])
+    second = halo[2, REACH]
+    known = [folded(halo[1, REACH], second), folded(second, second)]
     acc[...] = jnp.zeros_like(acc)
     add_product(2, REACH)
     within = acc[...]
     add_side(2, AHEAD)
     doubled = own_scale * (2.0 * acc[...] - within) + own_nugget * halo[2, REACH]
-    late1[place1] = as_row([folded(halo[2, REACH], doubled), jnp.zeros((128 - months, 128), F32)])
-    begin_sum(late1, sum_send.at[2], sum_recv.at[2])
-    hear(4)
-    pass_sum(sums1, sum_recv.at[0], sums2, sum_send.at[1], sum_recv.at[1])
+    pair[my_core] = as_row(
+        known + [folded(halo[2, REACH], doubled), jnp.zeros((128 - 3 * months, 128), F32)]
+    )
+    pair_copy = pltpu.make_async_remote_copy(
+        src_ref=pair.at[my_core], dst_ref=pair.at[my_core], send_sem=pair_sems.at[0], recv_sem=pair_sems.at[1],
+        device_id=(my_s + 1 - 2 * my_core, my_r), device_id_type=MESH,
+    )
+    pair_copy.start()
+    await_bytes(pair.at[0], pair_sems.at[1])
+    late[chip] = pair[0] + pair[1]
+    for ahead_z in swing(z_n):
+        for ahead_y in swing(y_n):
+            row = ((my_z + ahead_z) % z_n) * y_n + (my_y + ahead_y) % y_n
+            for ahead_r in swing(rep_n):
+                if ahead_z or ahead_y or ahead_r:
+                    pltpu.make_async_remote_copy(
+                        src_ref=late.at[chip], dst_ref=late.at[chip],
+                        send_sem=sum_send.at[2], recv_sem=sum_recv.at[2],
+                        device_id=(row * 2 + my_core, (my_r + ahead_r) % rep_n), device_id_type=MESH,
+                    ).start()
     add_side(2, BEHIND)
     last[my_r] = image_of(2)
     for step in range(1, rep_n):
@@ -317,31 +341,16 @@
             send_sem=last_send, recv_sem=last_recv.at[step],
             device_id=(my_s, (my_r + step) % rep_n), device_id_type=MESH,
         ).start()
-    pass_sum(late1, sum_recv.at[2], late2, sum_send.at[3], sum_recv.at[3])
-
-    total = end_sum(sums2, sum_recv.at[1])
-    m0, m1, m2, m3 = [total[at * months:(at + 1) * months, 0:1] for at in range(4)]
-    m4 = total[:months, 1:2]
+
+    def thirds(columns):
+        return [columns[at * months:(at + 1) * months, 0:1] for at in range(3)]
+
+    m0, m1, m2 = thirds(end_sum(sums2, sum_recv.at[1]))
     alpha0 = m0 / m1
     norm1 = alpha0 * alpha0 * m2 - m0
     lead = 1.0 + norm1 / m0
-    alpha1 = norm1 / (alpha0 * (alpha0 * m3 - lead * m2))
-    r1 = -(alpha0 + alpha1 * lead)
-    r2 = alpha0 * alpha1
-    norm2 = r2 * (m2 + r1 * m3 + r2 * m4)
-    beta2 = norm2 / norm1
-    d0 = 1.0 + beta2 * lead
-    d1 = r1 - beta2 * alpha0
     for step in range(1, rep_n):
         await_bytes(last.at[0], last_recv.at[step])
-    for place in range(rep_n):
-        lanes = slice(place * width, (place + 1) * width)
-        slot = REACH + place - my_r
-        start, first, second = halo[0, slot], halo[1, slot], halo[2, slot]
-        held[0, :, lanes] = (alpha0 + alpha1 * lead) * start - (alpha1 * alpha0) * first
-        held[1, :, lanes] = d0 * start + d1 * first + r2 * second
-        held[2, :, lanes] = start + r1 * first + r2 * second
-        held[3, :, lanes] = d0 * first + d1 * second + r2 * last[place]
     count = len(OFFSETS)
     await_bytes(geo.at[pl.ds(0, rep_n + 1)], geo_send)
     await_bytes(halo.at[0, pl.ds(0, rep_n + 1)], halo_send.at[0])
@@ -350,22 +359,34 @@
     await_bytes(last.at[pl.ds(0, rep_n - 1)], last_send)
     await_bytes(sums1.at[pl.ds(0, n1 - 1)], sum_send.at[0])
     await_bytes(sums2.at[pl.ds(0, n2 - 1)], sum_send.at[1])
-    await_bytes(late1.at[pl.ds(0, n1 - 1)], sum_send.at[2])
-
-    m5 = end_sum(late2, sum_recv.at[3])[:months, 0:1]
+
+    await_bytes(late.at[pl.ds(0, chain_n // 2 - 1)], sum_recv.at[2])
+    m3, m4, m5 = thirds(columns_of(jnp.sum(late[...], axis=0)))
+    alpha1 = norm1 / (alpha0 * (alpha0 * m3 - lead * m2))
+    r1 = -(alpha0 + alpha1 * lead)
+    r2 = alpha0 * alpha1
+    norm2 = r2 * (m2 + r1 * m3 + r2 * m4)
+    beta2 = norm2 / norm1
+    d0 = 1.0 + beta2 * lead
+    d1 = r1 - beta2 * alpha0
     alpha2 = norm2 / (r2 * (d0 * m3 + d1 * m4 + r2 * m5))
+    found = (alpha2 * d0 - r1, alpha2 * d1 - r2, alpha2 * r2)
+    left = (r1 - alpha2 * d0, r2 - alpha2 * d1, -alpha2 * r2)
     stores = []
     for place in range(rep_n):
         lanes = slice(place * width, (place + 1) * width)
-        made[0, :, lanes] = held[0, :, lanes] + alpha2 * held[1, :, lanes]
-        made[1, :, lanes] = held[2, :, lanes] - alpha2 * held[3, :, lanes]
+        slot = REACH + place - my_r
+        start, first, second = halo[0, slot], halo[1, slot], halo[2, slot]
+        made[0, :, lanes] = found[0] * start + found[1] * first + found[2] * second
+        made[1, :, lanes] = start + left[0] * first + left[1] * second + left[2] * last[place]
         for which, out in enumerate((out_solution, out_residual)):
             store = pltpu.make_async_copy(made.at[which, :, lanes], out.at[:, lanes], out_sem.at[which, place])
             store.start()
             stores.append(store)
     for store in stores:
         store.wait()
-    await_bytes(late2.at[pl.ds(0, n2 - 1)], sum_send.at[3])
+    await_bytes(late.at[pl.ds(0, chain_n // 2 - 1)], sum_send.at[2])
+    await_bytes(pair.at[0], pair_sems.at[0])
 
 
 def solution(mesh):
@@ -397,14 +418,13 @@
                 pltpu.VMEM((3, SLOTS, months, width), F32),
                 pltpu.VMEM((rep_n, months, width), F32),
                 pltpu.VMEM((months, width), F32),
-                pltpu.VMEM((rep_n * y_n, 2, 128), F32),
-                pltpu.VMEM((2 * z_n, 2, 128), F32),
                 pltpu.VMEM((rep_n * y_n, 1, 128), F32),
                 pltpu.VMEM((2 * z_n, 1, 128), F32),
-                pltpu.VMEM((4, months, group_width), F32),
+                pltpu.VMEM((sites_n * rep_n // 2, 1, 128), F32),
+                pltpu.VMEM((2, 1, 128), F32),
                 pltpu.VMEM((2, months, group_width), F32),
                 dma((5,)), dma((2, rep_n)), dma, dma((SLOTS,)), dma((3,)), dma((3, SLOTS)), dma, dma((rep_n,)),
-                dma((4,)), dma((4,)), pltpu.SemaphoreType.REGULAR((5,)),
+                dma((3,)), dma((3,)), dma((2,)), pltpu.SemaphoreType.REGULAR((5,)),
             ],
             compiler_params=pltpu.CompilerParams(
                 collective_id=0, has_side_effects=True, vmem_limit_bytes=56 * 2**20

time: 47.6 us -> 46.3 us (0.973)
  Pallas kernels: 44.4 us -> 43.1 us
    pallas_call x1, Pallas kernels: 44.4 us -> 43.1 us  [local(): pl.pallas_call(functools.partial(kernel, (sites_n, rep_n, z_n, y_n)), out...]
where the time goes in v5:
time: 46.3 us; the launch traced here: 46.2 us
  Pallas kernels  43.1 us (93%)
  local copies, waits for them, and re-layouts  2.42 us (5%)
  between operations  0.65 us (1%)
    pallas_call x1, Pallas kernels, local(): pl.pallas_call(functools.partial(kernel, (sites_n, rep_n, z_n, y_n)), out...  43.1 us
    unnamed x4, local copies, waits for them, and re-layouts  2.42 us

profile of v5, /device:TPU:1, one launch (start us, length us, event | category | flops | bytes accessed | tf_op | source)
XLA Modules:
  0.0 46.2 jit_solution(648078647888647507)
XLA Ops:
  0.6 43.1 %shard_map.68 = (f32[32,2048]{1,0:T(8,128)}, f32[32,2048]{1,0:T(8,128)}) custom-call(f32[2,2048]{1,0:T(2,128)} %coords_in.1, f32[1,2048]{1,0:T(1,128)} %bitcast.3, f32[1,2048]{1,0:T(1,128)} %bitcast.4, f32[32,2048]{1,0:T(8,128)} %right_side_in.1, s32[1,2048]{1,0:T(1,128)} %bitcast.5), custom_call_target="tpu_custom_call" | custom-call | tf_op jit(solution)/shard_map/pallas_call | solution.py:403
  43.7 0.0 copy-start
  43.7 1.7 %copy.9 = f32[32,2048]{1,0:T(8,128)} copy(f32[32,2048]{1,0:T(8,128)} %get-tuple-element.4) | data formatting | bytes 524288
  45.5 0.0 copy-done
  45.5 0.7 %copy.10 = f32[32,2048]{1,0:T(8,128)} copy(f32[32,2048]{1,0:T(8,128)S(1)} %copy-done) | data formatting | bytes 524288
Async XLA Ops:
  43.7 1.7 %copy-start = (f32[32,2048]{1,0:T(8,128)S(1)}, f32[32,2048]{1,0:T(8,128)}, u32[]{:S(2)}) copy-start(f32[32,2048]{1,0:T(8,128)} %get-tuple-element.5) | copy-start | bytes 786436

commit v6 on v5

--- a/solution.py
+++ b/solution.py
@@ -35,8 +35,8 @@
     coords_in, scale_in, nugget_in, right_side_in, order_in,
     out_solution, out_residual,
     coords, scale, nugget, right_side, order,
-    data, tile_high, tile_low, geo, halo, last, acc, sums1, sums2, late, pair, made,
-    in_sems, out_sem, geo_send, geo_recv, halo_send, halo_recv, last_send, last_recv,
+    data, tile_high, tile_low, geo, halo, last, acc, sums1, sums2, late, pair,
+    in_sems, geo_send, geo_recv, halo_send, halo_recv, last_send, last_recv,
     sum_send, sum_recv, pair_sems, told,
 ):
     sites_n, rep_n, z_n, y_n = sizes
@@ -221,24 +221,26 @@
     def come_slot(turn):
         return jnp.where(upward(turn), turn, REACH + turn)
 
-    def other_tiles(turn, carry):
+    def come_product(slot):
+        await_bytes(halo.at[0, slot], halo_recv.at[0, slot])
+        add_product(0, slot)
+
+    def other_pieces(turn, carry):
         slot = come_slot(turn)
         await_bytes(geo.at[slot], geo_recv.at[slot])
+        come_product(come_slot(turn - 1))
         make_tiles(slot, False)
         return carry
 
     await_bytes(geo.at[0], geo_recv.at[0])
     make_tiles(0, False, (0, width - step_rows))
-    lax.fori_loop(1, rep_n, other_tiles, 0)
+    lax.fori_loop(1, rep_n, other_pieces, 0)
     await_bytes(geo.at[2 * REACH], geo_recv.at[2 * REACH])
+    come_product(come_slot(rep_n - 1))
     make_tiles(2 * REACH, False, (width - step_rows, 0))
+    come_product(2 * REACH)
     hear(1)
     tell(2)
-    for turn in range(rep_n + 1):
-        slot = come_slot(turn)
-        await_bytes(halo.at[0, slot], halo_recv.at[0, slot])
-        add_product(0, slot)
-
     def spread_halo(stage):
         for offset in OFFSETS:
             pltpu.make_async_remote_copy(
@@ -372,19 +374,12 @@
     alpha2 = norm2 / (r2 * (d0 * m3 + d1 * m4 + r2 * m5))
     found = (alpha2 * d0 - r1, alpha2 * d1 - r2, alpha2 * r2)
     left = (r1 - alpha2 * d0, r2 - alpha2 * d1, -alpha2 * r2)
-    stores = []
     for place in range(rep_n):
         lanes = slice(place * width, (place + 1) * width)
         slot = REACH + place - my_r
         start, first, second = halo[0, slot], halo[1, slot], halo[2, slot]
-        made[0, :, lanes] = found[0] * start + found[1] * first + found[2] * second
-        made[1, :, lanes] = start + left[0] * first + left[1] * second + left[2] * last[place]
-        for which, out in enumerate((out_solution, out_residual)):
-            store = pltpu.make_async_copy(made.at[which, :, lanes], out.at[:, lanes], out_sem.at[which, place])
-            store.start()
-            stores.append(store)
-    for store in stores:
-        store.wait()
+        out_solution[:, lanes] = found[0] * start + found[1] * first + found[2] * second
+        out_residual[:, lanes] = start + left[0] * first + left[1] * second + left[2] * last[place]
     await_bytes(late.at[pl.ds(0, chain_n // 2 - 1)], sum_send.at[2])
     await_bytes(pair.at[0], pair_sems.at[0])
 
@@ -404,7 +399,7 @@
             functools.partial(kernel, (sites_n, rep_n, z_n, y_n)),
             out_shape=(out, out),
             in_specs=[anywhere] * 5,
-            out_specs=(anywhere, anywhere),
+            out_specs=(pl.BlockSpec(memory_space=pltpu.VMEM),) * 2,
             scratch_shapes=[
                 pltpu.VMEM((2, group_width), F32),
                 pltpu.VMEM((1, group_width), F32),
@@ -422,8 +417,7 @@
                 pltpu.VMEM((2 * z_n, 1, 128), F32),
                 pltpu.VMEM((sites_n * rep_n // 2, 1, 128), F32),
                 pltpu.VMEM((2, 1, 128), F32),
-                pltpu.VMEM((2, months, group_width), F32),
-                dma((5,)), dma((2, rep_n)), dma, dma((SLOTS,)), dma((3,)), dma((3, SLOTS)), dma, dma((rep_n,)),
+                dma((5,)), dma, dma((SLOTS,)), dma((3,)), dma((3, SLOTS)), dma, dma((rep_n,)),
                 dma((3,)), dma((3,)), dma((2,)), pltpu.SemaphoreType.REGULAR((5,)),
             ],
             compiler_params=pltpu.CompilerParams(

time: 46.3 us -> 45.5 us (0.983)
  Pallas kernels: 43.1 us -> 42.3 us
    pallas_call x1, Pallas kernels: 43.1 us -> 42.3 us  [local(): pl.pallas_call(functools.partial(kernel, (sites_n, rep_n, z_n, y_n)), out...]
where the time goes in v6:
time: 45.5 us; the launch traced here: 45.4 us
  Pallas kernels  42.3 us (93%)
  local copies, waits for them, and re-layouts  2.42 us (5%)
  between operations  0.65 us (1%)
    pallas_call x1, Pallas kernels, local(): pl.pallas_call(functools.partial(kernel, (sites_n, rep_n, z_n, y_n)), out...  42.3 us
    unnamed x4, local copies, waits for them, and re-layouts  2.42 us

profile of v6, /device:TPU:1, one launch (start us, length us, event | category | flops | bytes accessed | tf_op | source)
XLA Modules:
  0.0 45.4 jit_solution(177455077022017402)
XLA Ops:
  0.6 42.3 %shard_map.68 = (f32[32,2048]{1,0:T(8,128)}, f32[32,2048]{1,0:T(8,128)}) custom-call(f32[2,2048]{1,0:T(2,128)} %coords_in.1, f32[1,2048]{1,0:T(1,128)} %bitcast.3, f32[1,2048]{1,0:T(1,128)} %bitcast.4, f32[32,2048]{1,0:T(8,128)} %right_side_in.1, s32[1,2048]{1,0:T(1,128)} %bitcast.5), custom_call_target="tpu_custom_call" | custom-call | tf_op jit(solution)/shard_map/pallas_call | solution.py:398
  42.9 0.0 copy-start
  43.0 1.7 %copy.9 = f32[32,2048]{1,0:T(8,128)} copy(f32[32,2048]{1,0:T(8,128)} %get-tuple-element.4) | data formatting | bytes 524288
  44.7 0.0 copy-done
  44.7 0.7 %copy.10 = f32[32,2048]{1,0:T(8,128)} copy(f32[32,2048]{1,0:T(8,128)S(1)} %copy-done) | data formatting | bytes 524288
Async XLA Ops:
  42.9 1.7 %copy-start = (f32[32,2048]{1,0:T(8,128)S(1)}, f32[32,2048]{1,0:T(8,128)}, u32[]{:S(2)}) copy-start(f32[32,2048]{1,0:T(8,128)} %get-tuple-element.5) | copy-start | bytes 786436

commit v7 on v6

--- a/solution.py
+++ b/solution.py
@@ -33,7 +33,7 @@
 def kernel(
     sizes,
     coords_in, scale_in, nugget_in, right_side_in, order_in,
-    out_solution, out_residual,
+    out,
     coords, scale, nugget, right_side, order,
     data, tile_high, tile_low, geo, halo, last, acc, sums1, sums2, late, pair,
     in_sems, geo_send, geo_recv, halo_send, halo_recv, last_send, last_recv,
@@ -378,8 +378,8 @@
         lanes = slice(place * width, (place + 1) * width)
         slot = REACH + place - my_r
         start, first, second = halo[0, slot], halo[1, slot], halo[2, slot]
-        out_solution[:, lanes] = found[0] * start + found[1] * first + found[2] * second
-        out_residual[:, lanes] = start + left[0] * first + left[1] * second + left[2] * last[place]
+        out[0, :, lanes] = found[0] * start + found[1] * first + found[2] * second
+        out[1, :, lanes] = start + left[0] * first + left[1] * second + left[2] * last[place]
     await_bytes(late.at[pl.ds(0, chain_n // 2 - 1)], sum_send.at[2])
     await_bytes(pair.at[0], pair_sems.at[0])
 
@@ -394,12 +394,11 @@
         width = group_width // rep_n
         anywhere = pl.BlockSpec(memory_space=pl.ANY)
         dma = pltpu.SemaphoreType.DMA
-        out = jax.ShapeDtypeStruct((months, group_width), F32)
-        return pl.pallas_call(
+        both = pl.pallas_call(
             functools.partial(kernel, (sites_n, rep_n, z_n, y_n)),
-            out_shape=(out, out),
+            out_shape=jax.ShapeDtypeStruct((2, months, group_width), F32),
             in_specs=[anywhere] * 5,
-            out_specs=(pl.BlockSpec(memory_space=pltpu.VMEM),) * 2,
+            out_specs=pl.BlockSpec(memory_space=pltpu.VMEM),
             scratch_shapes=[
                 pltpu.VMEM((2, group_width), F32),
                 pltpu.VMEM((1, group_width), F32),
@@ -424,6 +423,7 @@
                 collective_id=0, has_side_effects=True, vmem_limit_bytes=56 * 2**20
             ),
         )(coords, scale[None, :], nugget[None, :], right_side, site_order[None, :])
+        return (both[0], both[1])
 
     in_specs = (
         P(None, "sites"),

time: 45.5 us -> 44.9 us (0.987)
  local copies, waits for them, and re-layouts: 2.42 us -> 1.86 us
    unnamed x4 -> x0, local copies, waits for them, and re-layouts: 2.42 us -> none
    squeeze x0 -> x1, local copies, waits for them, and re-layouts: none -> 1.86 us  [local(): return (both[0], both[1])]
where the time goes in v7:
time: 44.9 us; the launch traced here: 44.8 us
  Pallas kernels  42.3 us (94%)
  local copies, waits for them, and re-layouts  1.86 us (4%)
  between operations  0.64 us (1%)
    pallas_call x1, Pallas kernels, local(): pl.pallas_call(functools.partial(kernel, (sites_n, rep_n, z_n, y_n)), out...  42.3 us
    squeeze x1, local copies, waits for them, and re-layouts, local(): return (both[0], both[1])  1.86 us

profile of v7, /device:TPU:1, one launch (start us, length us, event | category | flops | bytes accessed | tf_op | source)
XLA Modules:
  0.0 44.8 jit_solution(2101004497718772134)
XLA Ops:
  0.6 42.3 %shard_map.68 = f32[2,32,2048]{2,1,0:T(8,128)} custom-call(f32[2,2048]{1,0:T(2,128)} %coords_in.1, f32[1,2048]{1,0:T(1,128)} %bitcast.7, f32[1,2048]{1,0:T(1,128)} %bitcast.8, f32[32,2048]{1,0:T(8,128)} %right_side_in.1, s32[1,2048]{1,0:T(1,128)} %bitcast.9), custom_call_target="tpu_custom_call" | custom-call | tf_op jit(solution)/shard_map/pallas_call | solution.py:397
  42.9 1.9 %slice_bitcast_fusion = (f32[32,2048]{1,0:T(8,128)}, f32[32,2048]{1,0:T(8,128)}) fusion(f32[2,32,2048]{2,1,0:T(8,128)} %shard_map.68), kind=kLoop, calls=%fused_computation | loop fusion | bytes 1048576 | tf_op jit(solution)/shard_map/squeeze | solution.py:426

commit v8 on v7

--- a/solution.py
+++ b/solution.py
@@ -194,19 +194,21 @@
     def upward(turn):
         return turn <= rep_n - 1 - my_r
 
-    def exchange(ref_of, send_sem, recv_of):
-        for turn in range(rep_n + 1):
-            up = upward(turn)
-            source = jnp.where(up, REACH + turn, turn)
-            target = jnp.where(up, turn, REACH + turn)
-            group = (my_s + jnp.where(up, 1, sites_n - 1)) % sites_n
-            pltpu.make_async_remote_copy(
-                src_ref=ref_of(source), dst_ref=ref_of(target), send_sem=send_sem, recv_sem=recv_of(target),
-                device_id=(group, my_r), device_id_type=MESH,
-            ).start()
-
-    exchange(lambda slot: geo.at[slot], geo_send, lambda slot: geo_recv.at[slot])
-    exchange(lambda slot: halo.at[0, slot], halo_send.at[0], lambda slot: halo_recv.at[0, slot])
+    def exchange(turn, ref_of, send_sem, recv_of):
+        up = upward(turn)
+        source = jnp.where(up, REACH + turn, turn)
+        target = jnp.where(up, turn, REACH + turn)
+        group = (my_s + jnp.where(up, 1, sites_n - 1)) % sites_n
+        pltpu.make_async_remote_copy(
+            src_ref=ref_of(source), dst_ref=ref_of(target), send_sem=send_sem, recv_sem=recv_of(target),
+            device_id=(group, my_r), device_id_type=MESH,
+        ).start()
+
+    for turn in range(rep_n + 2):
+        if turn <= rep_n:
+            exchange(turn, lambda slot: geo.at[slot], geo_send, lambda slot: geo_recv.at[slot])
+        if turn >= 1:
+            exchange(turn - 1, lambda slot: halo.at[0, slot], halo_send.at[0], lambda slot: halo_recv.at[0, slot])
 
     acc[...] = jnp.zeros_like(acc)
 

time: 44.9 us -> 44.9 us (level)
  no operation moved by 1% of the time
where the time goes in v8:
time: 44.9 us; the launch traced here: 44.8 us
  Pallas kernels  42.3 us (94%)
  local copies, waits for them, and re-layouts  1.86 us (4%)
  between operations  0.64 us (1%)
    pallas_call x1, Pallas kernels, local(): pl.pallas_call(functools.partial(kernel, (sites_n, rep_n, z_n, y_n)), out...  42.3 us
    squeeze x1, local copies, waits for them, and re-layouts, local(): return (both[0], both[1])  1.86 us

profile of v8, /device:TPU:1, one launch (start us, length us, event | category | flops | bytes accessed | tf_op | source)
XLA Modules:
  0.0 44.8 jit_solution(16137128257681191438)
XLA Ops:
  0.6 42.3 %shard_map.68 = f32[2,32,2048]{2,1,0:T(8,128)} custom-call(f32[2,2048]{1,0:T(2,128)} %coords_in.1, f32[1,2048]{1,0:T(1,128)} %bitcast.7, f32[1,2048]{1,0:T(1,128)} %bitcast.8, f32[32,2048]{1,0:T(8,128)} %right_side_in.1, s32[1,2048]{1,0:T(1,128)} %bitcast.9), custom_call_target="tpu_custom_call" | custom-call | tf_op jit(solution)/shard_map/pallas_call | solution.py:399
  43.0 1.9 %slice_bitcast_fusion = (f32[32,2048]{1,0:T(8,128)}, f32[32,2048]{1,0:T(8,128)}) fusion(f32[2,32,2048]{2,1,0:T(8,128)} %shard_map.68), kind=kLoop, calls=%fused_computation | loop fusion | bytes 1048576 | tf_op jit(solution)/shard_map/squeeze | solution.py:428
